TPU v7x, 32 devices: a whole 2x2x4 slice. The times are simulated.
32 devices in a mesh: seq: 8 (over z, y), dp: 4 (over x, core).
Axes of the slice: x: 2, y: 2, z: 4, core: 2. Of those that a mesh axis runs over, the one named last changes fastest.
Arguments:
- tokens: int32 [4, 1024], P('dp', 'seq'), may hold values from 65 to 116, as said below
- embed: bfloat16 [512, 1536], replicated, may hold values from -6 to 6
- taps: float32 [3, 3, 512], replicated, may hold values from -3.5 to 3.5
- skip: float32 [512], replicated, may hold values from -4 to 4
- rates: float32 [512], replicated, may hold values from 0.3 to 34
- w_one: float32 [128, 128], replicated, may hold values from -0.5 to 0.5
- b_one: float32 [128], replicated, may hold values from -4 to 4
- w_two: float32 [128, 128], replicated, may hold values from -0.5 to 0.5
- b_two: float32 [128], replicated, may hold values from -4 to 4
- w_three: float32 [128, 512], replicated, may hold values from -0.5 to 0.5
- cotangent: bfloat16 [4, 1024, 512], P('dp', 'seq'), may hold values from -0.029907227 to 0.029907227
Outputs:
- gated: bfloat16 [4, 1024, 512], P('dp', 'seq')
- grad_w_one: float32 [128, 128], replicated
- grad_b_one: float32 [128], replicated
- grad_w_two: float32 [128, 128], replicated
- grad_b_two: float32 [128], replicated
- grad_w_three: float32 [128, 512], replicated
Inputs may be any that keep to these rules, and one draw needn't show every extreme that they name: `tokens`: byte codes of the letters A, C, G, T, their lower-case forms, N and n.
All inputs are finite; a program needn't handle non-finite values.
Results may differ from a plain program's by a relative error of at most 0.001.
Values sent between devices are 32-bit elements; how exact they have to be, the bound alone decides.
No kernel may reach another device: no remote copies, remote signals or barrier semaphores. Data moves between devices by JAX's collectives and lax.ppermute only.
A program may use at most 64 MiB of HBM per device.

v0:
```python
import math

import jax
import jax.numpy as jnp
from jax import lax
from jax.sharding import PartitionSpec as P

full_turn = 2.0 * math.pi
precise = lax.Precision.HIGHEST


def passed_along(block, axis, distance):
    devices = range(lax.axis_size(axis))
    route = [(i - distance, i) for i in devices if i - distance in devices]
    return lax.ppermute(block, axis, route)


def band_numbers(length, band_count):
    return [
        max(band_index + 1, int(0.4 * length ** (band_index / (band_count - 1))))
        for band_index in range(band_count)
    ]


def position_features(positions, length, band_count):
    numbers = jnp.array(band_numbers(length, band_count), dtype=jnp.int32)
    upper_part = positions[:, None] // 256
    lower_part = positions[:, None] % 256
    wrapped = 256 * numbers[None, :] % length
    residue = (upper_part * wrapped % length + lower_part * numbers[None, :]) % length
    angles = residue.astype(jnp.float32) * (full_turn / length)
    return jnp.concatenate([jnp.sin(angles), jnp.cos(angles)], axis=1)


def matmul(left, right):
    return jnp.dot(left, right, precision=precise, preferred_element_type=jnp.float32)


def phase_table(numerators, modulus):
    angles = (numerators % modulus).astype(jnp.float32) * (full_turn / modulus)
    return (jnp.cos(angles), jnp.sin(angles))


def fine_tables(row_count, devices):
    index_row = jnp.arange(row_count, dtype=jnp.int32)
    cosine, sine_part = phase_table(index_row[:, None] * index_row[None, :], row_count)
    shape_new = (devices, row_count // devices, row_count)
    return (cosine.reshape(shape_new), sine_part.reshape(shape_new))


def real_blocks(blocks):
    return lax.all_to_all(blocks, "seq", split_axis=1, concat_axis=1, tiled=True)


def spectral_blocks(spectra):
    return lax.all_to_all(spectra, "seq", split_axis=2, concat_axis=2, tiled=True)


def forward_transform(signal):
    devices = lax.axis_size("seq")
    own_index = lax.axis_index("seq")
    seq_count = signal.shape[0]
    row_count = signal.shape[1]
    chan_count = signal.shape[2]
    per_slot = row_count // devices
    period = 2 * row_count * devices
    columns = real_blocks(signal.reshape(seq_count, devices, per_slot, chan_count))
    source = jnp.arange(devices, dtype=jnp.int32)
    offset = jnp.arange(per_slot, dtype=jnp.int32)
    coarse = jnp.arange(2 * devices, dtype=jnp.int32)
    position = source[None, None, :] * row_count + own_index * per_slot + offset[:, None, None]
    cosine, sine_part = phase_table(coarse[None, :, None] * position, period)
    phases = jnp.stack([cosine, -sine_part])
    mixture = jnp.einsum(
        "rbkp,npbc->nrkbc", phases, columns, precision=precise, preferred_element_type=jnp.float32
    )
    spectra = spectral_blocks(mixture.reshape(seq_count, 2, devices, 2, per_slot, chan_count))
    cos_fine, sin_fine = fine_tables(row_count, devices)
    with_cos = jnp.einsum(
        "nrqsbc,qbk->nrskc",
        spectra,
        cos_fine,
        precision=precise,
        preferred_element_type=jnp.float32,
    )
    with_sin = jnp.einsum(
        "nrqsbc,qbk->nrskc",
        spectra,
        sin_fine,
        precision=precise,
        preferred_element_type=jnp.float32,
    )
    return jnp.stack([with_cos[:, 0] + with_sin[:, 1], with_cos[:, 1] - with_sin[:, 0]], axis=1)


def inverse_transform(spectrum):
    devices = lax.axis_size("seq")
    own_index = lax.axis_index("seq")
    seq_count = spectrum.shape[0]
    row_count = spectrum.shape[3]
    chan_count = spectrum.shape[4]
    per_slot = row_count // devices
    period = 2 * row_count * devices
    cos_fine, sin_fine = fine_tables(row_count, devices)
    with_cos = jnp.einsum(
        "nrskc,qbk->nrqsbc",
        spectrum,
        cos_fine,
        precision=precise,
        preferred_element_type=jnp.float32,
    )
    with_sin = jnp.einsum(
        "nrskc,qbk->nrqsbc",
        spectrum,
        sin_fine,
        precision=precise,
        preferred_element_type=jnp.float32,
    )
    value_real = with_cos[:, 0] - with_sin[:, 1]
    value_imag = with_sin[:, 0] + with_cos[:, 1]
    slot_index = (
        jnp.arange(devices, dtype=jnp.int32)[:, None, None] * per_slot
        + jnp.arange(per_slot, dtype=jnp.int32)[None, None, :]
    )
    coarse = 2 * own_index + jnp.arange(2, dtype=jnp.int32)[None, :, None]
    cosine, sine_part = phase_table(slot_index * coarse, period)
    cosine = cosine[None, :, :, :, None]
    sine_part = sine_part[None, :, :, :, None]
    twisted = jnp.stack(
        [
            value_real * cosine - value_imag * sine_part,
            value_real * sine_part + value_imag * cosine,
        ],
        axis=1,
    )
    gathered = spectral_blocks(twisted)
    target = jnp.arange(devices, dtype=jnp.int32)
    block_index = jnp.arange(devices, dtype=jnp.int32)[:, None, None]
    half_index = jnp.arange(2, dtype=jnp.int32)[None, :, None]
    cos_coarse, sin_coarse = phase_table(
        target[None, None, :] * (2 * block_index + half_index), 2 * devices
    )
    weights = jnp.stack([cos_coarse, -sin_coarse]) * (1.0 / period)
    spatial = jnp.einsum(
        "nrmsbc,rmsa->nabc",
        gathered,
        weights,
        precision=precise,
        preferred_element_type=jnp.float32,
    )
    return real_blocks(spatial).reshape(seq_count, row_count, chan_count)


def featurize(tokens, embed, taps):
    own_index = lax.axis_index("seq")
    row_count = tokens.shape[1]
    reach = taps.shape[1] - 1
    chan_count = taps.shape[2]
    vocabulary = embed.shape[0]
    rim = passed_along(tokens[:, row_count - reach :], "seq", 1)
    extended = jnp.concatenate([rim, tokens], axis=1)
    global_place = own_index * row_count - reach + jnp.arange(row_count + reach, dtype=jnp.int32)
    present = (global_place >= 0).astype(jnp.float32)
    one_hot = (
        extended[:, :, None] == jnp.arange(vocabulary, dtype=jnp.int32)[None, None, :]
    ).astype(jnp.bfloat16)
    looked = (
        jnp.einsum("nrv,vd->nrd", one_hot, embed, preferred_element_type=jnp.float32)
        * present[None, :, None]
    )
    outputs = []
    for branch_index in range(3):
        total = jnp.zeros((tokens.shape[0], row_count, chan_count), jnp.float32)
        for tap_index in range(reach + 1):
            begin = reach - tap_index
            total = (
                total
                + taps[branch_index, tap_index][None, None, :]
                * looked[
                    :,
                    begin : begin + row_count,
                    branch_index * chan_count : (branch_index + 1) * chan_count,
                ]
            )
        outputs.append(total)
    return (outputs[0], outputs[1], outputs[2])


def complex_times(left, right):
    return jnp.stack(
        [
            left[:, 0] * right[:, 0] - left[:, 1] * right[:, 1],
            left[:, 0] * right[:, 1] + left[:, 1] * right[:, 0],
        ],
        axis=1,
    )


def conj_times(left, right):
    return jnp.stack(
        [
            left[:, 0] * right[:, 0] + left[:, 1] * right[:, 1],
            left[:, 0] * right[:, 1] - left[:, 1] * right[:, 0],
        ],
        axis=1,
    )


def body(tokens, embed, taps, skip, rates, w_one, b_one, w_two, b_two, w_three, cotangent):
    devices = lax.axis_size("seq")
    own_index = lax.axis_index("seq")
    row_count = tokens.shape[1]
    chan_count = skip.shape[0]
    length = row_count * devices
    query, keyed, valued = featurize(tokens, embed, taps)
    signal = keyed * valued
    upstream = cotangent.astype(jnp.float32) * query
    positions = own_index * row_count + jnp.arange(row_count, dtype=jnp.int32)
    features = position_features(positions, length, w_one.shape[0] // 2)
    pre_one = matmul(features, w_one) + b_one
    act_one = jnp.sin(pre_one)
    pre_two = matmul(act_one, w_two) + b_two
    act_two = jnp.sin(pre_two)
    window = jnp.exp(-rates[None, :] * (positions.astype(jnp.float32) / length)[:, None]) * (
        1.0 / math.sqrt(length)
    )
    share_width = chan_count // lax.axis_size("dp")
    share_start = lax.axis_index("dp") * share_width
    three_share = lax.dynamic_slice_in_dim(w_three, share_start, share_width, 1)
    taps_local = matmul(act_two, three_share) * lax.dynamic_slice_in_dim(
        window, share_start, share_width, 1
    )
    taps_width = taps_local.shape[1]
    stacked_taps = taps_local[None]
    spectrum_all = forward_transform(jnp.concatenate([signal, stacked_taps], axis=2))
    spectrum_signal = spectrum_all[..., :chan_count]
    taps_part = spectrum_all[..., chan_count : chan_count + taps_width]
    spectrum_taps = lax.all_gather(taps_part, "dp", axis=4, tiled=True)
    product = complex_times(spectrum_signal, spectrum_taps)
    convolved = inverse_transform(product)
    gated = (query * (convolved + skip[None, None, :] * signal)).astype(jnp.bfloat16)
    spectrum_up = forward_transform(upstream)
    cross = conj_times(spectrum_signal, spectrum_up)
    lagged = inverse_transform(cross)
    slopes = jnp.sum(lagged, axis=0) * window
    grad_three = matmul(act_two.T, slopes)
    back_two = matmul(slopes, w_three.T) * jnp.cos(pre_two)
    grad_two = matmul(act_one.T, back_two)
    bias_two = jnp.sum(back_two, axis=0)
    back_one = matmul(back_two, w_two.T) * jnp.cos(pre_one)
    grad_one = matmul(features.T, back_one)
    bias_one = jnp.sum(back_one, axis=0)
    summed = lax.psum((grad_one, bias_one, grad_two, bias_two, grad_three), ("seq", "dp"))
    return (gated, summed[0], summed[1], summed[2], summed[3], summed[4])


def solution(mesh):
    return jax.shard_map(
        body,
        mesh=mesh,
        in_specs=(
            P("dp", "seq"),
            P(),
            P(),
            P(),
            P(),
            P(),
            P(),
            P(),
            P(),
            P(),
            P("dp", "seq", None),
        ),
        out_specs=(P("dp", "seq", None), P(), P(), P(), P(), P()),
        check_vma=False,
    )
```

profile of v0, /device:TPU:0, one launch (start us, length us, event | category | flops | bytes accessed | tf_op | source)
XLA Modules:
  0.0 356.0 jit_solution(14123114766279563572)
XLA Ops:
  8.0 4.9 %collective-permute-start = (s32[1,2]{1,0:T(1,128)S(1)}, s32[1,2]{1,0:T(1,128)S(1)}, u32[]{:S(2)}, u32[]{:S(2)}) collective-permute-start(s32[1,2]{1,0:T(1,128)S(1)} %slice.134), channel_id=1, source_target_pairs={{0,4},{4,8},{8,12},{12,16},{16,20},{20,24},{24,28},{1,5},{5,9},{9,... | collective-permute-start | bytes 32 | tf_op jit(solution)/shard_map/ppermute | solution.py:15
  23.0 4.9 %all-to-all-start = ((f32[1,8,16,640]{3,2,0,1:T(8,128)}), f32[1,8,16,640]{3,2,0,1:T(8,128)S(1)}, u32[]{:S(2)}, u32[]{:S(2)}) async-start(f32[1,8,16,640]{3,2,0,1:T(8,128)} %pad_maximum_fusion), calls=%async_computation | async-start | bytes 655360 | tf_op jit(solution)/shard_map/all_to_all | solution.py:52
  27.9 10.0 %all-to-all-done = f32[1,8,16,640]{3,2,0,1:T(8,128)S(1)} async-done(((f32[1,8,16,640]{3,2,0,1:T(8,128)}), f32[1,8,16,640]{3,2,0,1:T(8,128)S(1)}, u32[]{:S(2)}, u32[]{:S(2)}) %all-to-all-start) | async-done | bytes 327712 | tf_op jit(solution)/shard_map/all_to_all | solution.py:52
  37.9 4.1 %all-to-all-start.4 = ((f32[1,8,16,512]{3,2,0,1:T(8,128)}), f32[1,8,16,512]{3,2,0,1:T(8,128)}, u32[]{:S(2)}, u32[]{:S(2)}) async-start(f32[1,8,16,512]{3,2,0,1:T(8,128)} %bitcast.62), calls=%async_computation.4 | async-start | bytes 524288 | tf_op jit(solution)/shard_map/all_to_all | solution.py:52
  46.1 3.2 copy.30
  50.3 5.0 %all-to-all-start.1 = ((f32[1,2,8,2,16,640]{5,4,3,1,0,2:T(8,128)}), f32[1,2,8,2,16,640]{5,4,3,1,0,2:T(8,128)S(1)}, u32[]{:S(2)}, u32[]{:S(2)}) async-start(f32[1,2,8,2,16,640]{5,4,3,1,0,2:T(8,128)} %copy.30), calls=%async_computation.1 | async-start | bytes 2621440 | tf_op jit(solution)/shard_map/all_to_all | solution.py:56
  55.3 3.1 convolution_bitcast_fusion.3
  58.4 2.8 reshape.622
  61.2 2.8 copy.37
  64.0 21.5 %all-to-all-done.1 = f32[1,2,8,2,16,640]{5,4,3,1,0,2:T(8,128)S(1)} async-done(((f32[1,2,8,2,16,640]{5,4,3,1,0,2:T(8,128)}), f32[1,2,8,2,16,640]{5,4,3,1,0,2:T(8,128)S(1)}, u32[]{:S(2)}, u32[]{:S(2)}) %all-to-all-start.1) | async-done | bytes 1310752 | tf_op jit(solution)/shard_map/all_to_all | solution.py:56
  85.5 4.2 %all-to-all-start.5 = ((f32[1,2,8,2,16,512]{5,4,3,1,0,2:T(8,128)}), f32[1,2,8,2,16,512]{5,4,3,1,0,2:T(8,128)}, u32[]{:S(2)}, u32[]{:S(2)}) async-start(f32[1,2,8,2,16,512]{5,4,3,1,0,2:T(8,128)} %copy.37), calls=%async_computation.5 | async-start | bytes 2097152 | tf_op jit(solution)/shard_map/all_to_all | solution.py:56
  94.3 20.9 %all-to-all-done.5 = f32[1,2,8,2,16,512]{5,4,3,1,0,2:T(8,128)} async-done(((f32[1,2,8,2,16,512]{5,4,3,1,0,2:T(8,128)}), f32[1,2,8,2,16,512]{5,4,3,1,0,2:T(8,128)}, u32[]{:S(2)}, u32[]{:S(2)}) %all-to-all-start.5) | async-done | bytes 1048608 | tf_op jit(solution)/shard_map/all_to_all | solution.py:56
  115.2 2.6 convolution_bitcast_fusion.6
  117.8 2.6 convolution_bitcast_fusion.7
  131.9 3.8 %all-to-all-start.6 = ((f32[1,2,8,2,16,512]{5,4,3,1,0,2:T(8,128)}), f32[1,2,8,2,16,512]{5,4,3,1,0,2:T(8,128)S(1)}, u32[]{:S(2)}, u32[]{:S(2)}) async-start(f32[1,2,8,2,16,512]{5,4,3,1,0,2:T(8,128)} %maximum_bitcast_fusion.3), calls=%async_computation.6 | async-start | bytes 2097152 | tf_op jit(solution)/shard_map/all_to_all | solution.py:56
  138.0 23.3 %all-to-all-done.6 = f32[1,2,8,2,16,512]{5,4,3,1,0,2:T(8,128)S(1)} async-done(((f32[1,2,8,2,16,512]{5,4,3,1,0,2:T(8,128)}), f32[1,2,8,2,16,512]{5,4,3,1,0,2:T(8,128)S(1)}, u32[]{:S(2)}, u32[]{:S(2)}) %all-to-all-start.6) | async-done | bytes 1048608 | tf_op jit(solution)/shard_map/all_to_all | solution.py:56
  161.3 4.2 %all-to-all-start.2 = ((f32[1,2,8,2,16,512]{5,4,3,1,0,2:T(8,128)}), f32[1,2,8,2,16,512]{5,4,3,1,0,2:T(8,128)}, u32[]{:S(2)}, u32[]{:S(2)}) async-start(f32[1,2,8,2,16,512]{5,4,3,1,0,2:T(8,128)} %maximum_bitcast_fusion.1), calls=%async_computation.2 | async-start | bytes 2097152 | tf_op jit(solution)/shard_map/all_to_all | solution.py:56
  168.9 22.3 %all-to-all-done.2 = f32[1,2,8,2,16,512]{5,4,3,1,0,2:T(8,128)} async-done(((f32[1,2,8,2,16,512]{5,4,3,1,0,2:T(8,128)}), f32[1,2,8,2,16,512]{5,4,3,1,0,2:T(8,128)}, u32[]{:S(2)}, u32[]{:S(2)}) %all-to-all-start.2) | async-done | bytes 1048608 | tf_op jit(solution)/shard_map/all_to_all | solution.py:56
  191.1 3.4 all-to-all-start.7
  194.6 3.6 convolution_bitcast_fusion.11
  199.0 4.6 %all-to-all-done.7 = f32[1,8,16,512]{3,2,0,1:T(8,128)S(1)} async-done(((f32[1,8,16,512]{3,2,0,1:T(8,128)}), f32[1,8,16,512]{3,2,0,1:T(8,128)S(1)}, u32[]{:S(2)}, u32[]{:S(2)}) %all-to-all-start.7) | async-done | bytes 262176 | tf_op jit(solution)/shard_map/all_to_all | solution.py:52
  203.6 3.6 %all-to-all-start.3 = ((f32[1,8,16,512]{3,2,0,1:T(8,128)}), f32[1,8,16,512]{3,2,0,1:T(8,128)S(1)}, u32[]{:S(2)}, u32[]{:S(2)}) async-start(f32[1,8,16,512]{3,2,0,1:T(8,128)} %copy.34), calls=%async_computation.3 | async-start | bytes 524288 | tf_op jit(solution)/shard_map/all_to_all | solution.py:52
  211.4 40.9 %all-reduce = (f32[128]{0:T(128)}, f32[128]{0:T(128)}) all-reduce(f32[128]{0:T(128)S(1)} %get-tuple-element.47, f32[128]{0:T(128)S(1)} %get-tuple-element.49), channel_id=1, replica_groups=mesh['seq'=8,'dp'=4] {'seq','dp'}, use_global_device_ids=true, to_apply=%region_2.3 | all-reduce | flops 256 | bytes 2048 | tf_op jit(solution)/shard_map/psum | solution.py:253
  253.0 91.6 %all-reduce.4.cloned.1.call-done = (f32[128,128]{1,0:T(8,128)}, f32[128,128]{1,0:T(8,128)}, f32[128,512]{1,0:T(8,128)}) async-done(((f32[128,128]{1,0:T(8,128)}, f32[128,128]{1,0:T(8,128)}, f32[128,512]{1,0:T(8,128)}), (f32[128,128]{1,0:T(8,128)}, f32[128,128]{1,0:T(8,128)}, f32[128,512]{1,0:T(8,128)})) %all-reduce.4.cloned.1.call-update) | async-done | bytes 393232 | tf_op jit(solution)/shard_map/psum | solution.py:253
  (104 shorter events, 47.8 us)
Async XLA Ops:
  7.2 13.6 %copy-start = (bf16[512,1536]{1,0:T(8,128)(2,1)S(1)}, bf16[512,1536]{1,0:T(8,128)(2,1)}, u32[]{:S(2)}) copy-start(bf16[512,1536]{1,0:T(8,128)(2,1)} %param.13) | copy-start | bytes 4718596
  7.2 13.5 %copy-start.20 = (s32[1,128]{1,0:T(1,128)S(1)}, s32[1,128]{1,0:T(1,128)}, u32[]{:S(2)}) copy-start(s32[1,128]{1,0:T(1,128)} %param.12) | copy-start | bytes 1540
  8.0 12.6 %collective-permute-start = (s32[1,2]{1,0:T(1,128)S(1)}, s32[1,2]{1,0:T(1,128)S(1)}, u32[]{:S(2)}, u32[]{:S(2)}) collective-permute-start(s32[1,2]{1,0:T(1,128)S(1)} %slice.134), channel_id=1, source_target_pairs={{0,4},{4,8},{8,12},{12,16},{16,20},{20,24},{24,28},{1,5},{5,9},{9,... | collective-permute-start | bytes 32 | tf_op jit(solution)/shard_map/ppermute | solution.py:15
  23.0 14.9 %all-to-all-start = ((f32[1,8,16,640]{3,2,0,1:T(8,128)}), f32[1,8,16,640]{3,2,0,1:T(8,128)S(1)}, u32[]{:S(2)}, u32[]{:S(2)}) async-start(f32[1,8,16,640]{3,2,0,1:T(8,128)} %pad_maximum_fusion), calls=%async_computation | async-start | bytes 655360 | tf_op jit(solution)/shard_map/all_to_all | solution.py:52
  37.9 12.3 %all-to-all-start.4 = ((f32[1,8,16,512]{3,2,0,1:T(8,128)}), f32[1,8,16,512]{3,2,0,1:T(8,128)}, u32[]{:S(2)}, u32[]{:S(2)}) async-start(f32[1,8,16,512]{3,2,0,1:T(8,128)} %bitcast.62), calls=%async_computation.4 | async-start | bytes 524288 | tf_op jit(solution)/shard_map/all_to_all | solution.py:52
  49.3 6.0 %copy-start.5 = (f32[1,16,16,8]{2,3,0,1:T(8,128)S(1)}, f32[1,16,16,8]{2,3,0,1:T(8,128)}, u32[]{:S(2)}) copy-start(f32[1,16,16,8]{2,3,0,1:T(8,128)} %copy-done.4) | copy-start | bytes 24580
  50.3 35.3 %all-to-all-start.1 = ((f32[1,2,8,2,16,640]{5,4,3,1,0,2:T(8,128)}), f32[1,2,8,2,16,640]{5,4,3,1,0,2:T(8,128)S(1)}, u32[]{:S(2)}, u32[]{:S(2)}) async-start(f32[1,2,8,2,16,640]{5,4,3,1,0,2:T(8,128)} %copy.30), calls=%async_computation.1 | async-start | bytes 2621440 | tf_op jit(solution)/shard_map/all_to_all | solution.py:56
  85.5 29.7 %all-to-all-start.5 = ((f32[1,2,8,2,16,512]{5,4,3,1,0,2:T(8,128)}), f32[1,2,8,2,16,512]{5,4,3,1,0,2:T(8,128)}, u32[]{:S(2)}, u32[]{:S(2)}) async-start(f32[1,2,8,2,16,512]{5,4,3,1,0,2:T(8,128)} %copy.37), calls=%async_computation.5 | async-start | bytes 2097152 | tf_op jit(solution)/shard_map/all_to_all | solution.py:56
  89.8 35.5 %all-gather.2.cloned.1.call-start = ((), (), s32[]{:S(2)}) async-start(), calls=%async_computation.8 | async-start | bytes 1310720 | tf_op jit(solution)/shard_map/all_gather | solution.py:238
  131.9 29.4 %all-to-all-start.6 = ((f32[1,2,8,2,16,512]{5,4,3,1,0,2:T(8,128)}), f32[1,2,8,2,16,512]{5,4,3,1,0,2:T(8,128)S(1)}, u32[]{:S(2)}, u32[]{:S(2)}) async-start(f32[1,2,8,2,16,512]{5,4,3,1,0,2:T(8,128)} %maximum_bitcast_fusion.3), calls=%async_computation.6 | async-start | bytes 2097152 | tf_op jit(solution)/shard_map/all_to_all | solution.py:56
  161.3 29.8 %all-to-all-start.2 = ((f32[1,2,8,2,16,512]{5,4,3,1,0,2:T(8,128)}), f32[1,2,8,2,16,512]{5,4,3,1,0,2:T(8,128)}, u32[]{:S(2)}, u32[]{:S(2)}) async-start(f32[1,2,8,2,16,512]{5,4,3,1,0,2:T(8,128)} %maximum_bitcast_fusion.1), calls=%async_computation.2 | async-start | bytes 2097152 | tf_op jit(solution)/shard_map/all_to_all | solution.py:56
  191.1 12.5 %all-to-all-start.7 = ((f32[1,8,16,512]{3,2,0,1:T(8,128)}), f32[1,8,16,512]{3,2,0,1:T(8,128)S(1)}, u32[]{:S(2)}, u32[]{:S(2)}) async-start(f32[1,8,16,512]{3,2,0,1:T(8,128)} %copy.41), calls=%async_computation.7 | async-start | bytes 524288 | tf_op jit(solution)/shard_map/all_to_all | solution.py:52
  194.5 12.8 %copy-start.14 = (f32[128,512]{1,0:T(8,128)S(1)}, f32[128,512]{1,0:T(8,128)}, u32[]{:S(2)}) copy-start(f32[128,512]{1,0:T(8,128)} %param.21) | copy-start | bytes 786436
  194.5 12.8 %copy-start.16 = (f32[128,128]{1,0:T(8,128)S(1)}, f32[128,128]{1,0:T(8,128)}, u32[]{:S(2)}) copy-start(f32[128,128]{1,0:T(8,128)} %get-tuple-element.46) | copy-start | bytes 196612
  198.1 9.8 %copy-start.7 = (f32[128,128]{1,0:T(8,128)S(1)}, f32[128,128]{1,0:T(8,128)}, u32[]{:S(2)}) copy-start(f32[128,128]{1,0:T(8,128)} %copy-done.6) | copy-start | bytes 196612
  198.1 10.7 %copy-start.15 = (f32[128,128]{1,0:T(8,128)S(1)}, f32[128,128]{1,0:T(8,128)}, u32[]{:S(2)}) copy-start(f32[128,128]{1,0:T(8,128)} %get-tuple-element.44) | copy-start | bytes 196612
  198.1 10.7 %copy-start.17 = (f32[128,128]{1,0:T(8,128)S(1)}, f32[128,128]{1,0:T(8,128)}, u32[]{:S(2)}) copy-start(f32[128,128]{1,0:T(8,128)} %param.19) | copy-start | bytes 196612
  198.1 11.1 %copy-start.9 = (f32[128,64]{1,0:T(8,128)S(1)}, f32[128,64]{1,0:T(8,128)}, u32[]{:S(2)}) copy-start(f32[128,64]{1,0:T(8,128)} %copy-done.8) | copy-start | bytes 98308
  198.2 11.1 %copy-start.11 = (f32[128,64]{1,0:T(8,128)S(1)}, f32[128,64]{1,0:T(8,128)}, u32[]{:S(2)}) copy-start(f32[128,64]{1,0:T(8,128)} %copy-done.10) | copy-start | bytes 98308
  199.0 11.2 %copy-start.13 = (f32[128,128]{1,0:T(8,128)S(1)}, f32[128,128]{1,0:T(8,128)}, u32[]{:S(2)}) copy-start(f32[128,128]{1,0:T(8,128)} %copy-done.12) | copy-start | bytes 196612
  203.6 48.6 %all-to-all-start.3 = ((f32[1,8,16,512]{3,2,0,1:T(8,128)}), f32[1,8,16,512]{3,2,0,1:T(8,128)S(1)}, u32[]{:S(2)}, u32[]{:S(2)}) async-start(f32[1,8,16,512]{3,2,0,1:T(8,128)} %copy.34), calls=%async_computation.3 | async-start | bytes 524288 | tf_op jit(solution)/shard_map/all_to_all | solution.py:52
  207.2 137.3 %all-reduce.4.cloned.1.call-start = ((), (), s32[]{:S(2)}) async-start(), calls=%async_computation.9 | async-start | bytes 786432 | tf_op jit(solution)/shard_map/psum | solution.py:253
  207.3 44.9 %copy-start.3 = (f32[1,128,512]{2,1,0:T(8,128)S(1)}, f32[1,128,512]{2,1,0:T(8,128)}, u32[]{:S(2)}) copy-start(f32[1,128,512]{2,1,0:T(8,128)} %get-tuple-element.12) | copy-start | bytes 786436
  207.4 44.9 %copy-start.19 = (f32[512]{0:T(512)S(1)}, f32[512]{0:T(512)}, u32[]{:S(2)}) copy-start(f32[512]{0:T(512)} %param.15) | copy-start | bytes 6148
  (8 other events, 19.5 us)
Sparse Core Ops, SparseCore 0:
  94.2 17.9 all-gather.1
  214.3 130.2 all-reduce.3
where the time goes:
time: 358 us; the launch traced here: 356 us
  waiting for transfers between devices  195 us (54%)
  blocking collectives  40.9 us (11%)
  starting transfers between devices  38.3 us (11%)
  matrix products  34.8 us (10%)
  local copies, waits for them, and re-layouts  19.7 us (6%)
  between operations  14.5 us (4%)
  other arithmetic  12.6 us (4%)
    psum x1, waiting for transfers between devices, body(): lax.psum((grad_one, bias_one, grad_two, bias_two, grad_three), ('seq', 'd...  91.6 us
    all_to_all x4, waiting for transfers between devices, spectral_blocks(): lax.all_to_all(spectra, 'seq', split_axis=2, concat_axis=2, tiled=True)  88 us
    psum x1, blocking collectives, body(): lax.psum((grad_one, bias_one, grad_two, bias_two, grad_three), ('seq', 'd...  40.9 us
    all_to_all x4, starting transfers between devices, spectral_blocks(): lax.all_to_all(spectra, 'seq', split_axis=2, concat_axis=2, tiled=True)  17.3 us
    all_to_all x4, starting transfers between devices, real_blocks(): lax.all_to_all(blocks, 'seq', split_axis=1, concat_axis=1, tiled=True)  15.9 us
    all_to_all x4, waiting for transfers between devices, real_blocks(): lax.all_to_all(blocks, 'seq', split_axis=1, concat_axis=1, tiled=True)  15.6 us
    reshape x4, local copies, waits for them, and re-layouts, forward_transform(): mixture.reshape(seq_count, 2, devices, 2, per_slot, chan_count)  10.7 us
    dot_general x8, matrix products, matmul(): jnp.dot(left, right, precision=precise, preferred_element_type=jnp.float32)  8.81 us
  transfers between devices with their start and end apart: 11, of which 8 were waited for; matrix products, arithmetic and copies ran while one was open for 15% of the time, Pallas kernels for 0%

commit v1 on v0

v1 whole, which is shorter than its diff:
```python
import functools
import math

import jax
import jax.numpy as jnp
import ml_dtypes
import numpy as np
from jax import lax
from jax.experimental import pallas as pl
from jax.experimental.pallas import tpu as pltpu
from jax.sharding import PartitionSpec as P

LETTERS = (65, 67, 71, 84, 97, 99, 103, 116, 78, 110)
GROUP = 16
LANES = 128
CHUNK = 8
VMEM = 56 * 1024 * 1024
F32 = jnp.float32
BF16 = jnp.bfloat16


def halves(table):
    high = table.astype(np.float32).astype(ml_dtypes.bfloat16)
    low = (table - high.astype(np.float64)).astype(np.float32).astype(ml_dtypes.bfloat16)
    return high, low


def band_numbers(length, band_count):
    return [
        max(band + 1, int(0.4 * length ** (band / (band_count - 1)))) for band in range(band_count)
    ]


@functools.cache
def feature_tables(length, band_count):
    numbers = np.array(band_numbers(length, band_count), np.int64)
    residue = (numbers[:, None] * np.arange(length, dtype=np.int64)[None, :]) % length
    angles = residue * (2.0 * math.pi / length)
    return halves(np.concatenate([np.sin(angles), np.cos(angles)], axis=0))


@functools.cache
def transform_tables(rows):
    theta = np.pi * (np.arange(rows) + 0.5) / rows
    angles = np.arange(rows)[:, None] * theta[None, :]
    forward = np.concatenate([np.cos(angles), -np.sin(angles)], axis=1)
    high, low = halves(forward)
    first = np.concatenate([high, low], axis=0)
    inv_high, inv_low = halves(forward.T / rows)
    inverse = np.concatenate([inv_high, inv_low], axis=1)
    sign = np.broadcast_to(np.where(np.arange(rows) % 2 == 0, 1.0, -1.0), (8, rows))
    return first, inverse, sign.astype(np.float32)


@functools.cache
def letter_tables(lanes):
    code = np.full((lanes,), -1, np.int32)
    pick = np.zeros((lanes, lanes), np.float32)
    for row in range(6 * GROUP):
        if row % GROUP < len(LETTERS):
            code[row] = LETTERS[row % GROUP]
            pick[row, code[row]] = 1.0
    code = np.ascontiguousarray(np.broadcast_to(code[:, None], (lanes, lanes)))
    return code, pick.astype(ml_dtypes.bfloat16)


def split(x):
    high = x.astype(BF16)
    return high, (x - high.astype(F32)).astype(BF16)


def mm(a, b, ca=1, cb=0):
    return lax.dot_general(a, b, (((ca,), (cb,)), ((), ())), preferred_element_type=F32)


def left_mm(stack, high, low, cb=0):
    m = stack.shape[0] // 2
    both = mm(stack, high, cb=cb)
    return both[:m] + both[m:] + mm(stack[:m], low, cb=cb)


def sin_cos(x):
    turns = jnp.floor(x * (2.0 / math.pi) + 0.5)
    r = x - turns * 1.5703125
    r = r - turns * 4.837512969970703125e-4
    r = r - turns * 7.549789948768648e-8
    quarter = turns.astype(jnp.int32)
    z = r * r
    s = r + r * z * (-1.6666654611e-1 + z * (8.3321608736e-3 + z * -1.9515295891e-4))
    c = 1.0 + z * (
        -0.5 + z * (4.166664568298827e-2 + z * (-1.388731625493765e-3 + z * 2.443315711809948e-5))
    )
    swap = (quarter & 1) == 1
    sine = jnp.where(swap, c, s)
    cosine = jnp.where(swap, s, c)
    sine = jnp.where((quarter & 2) == 2, -sine, sine)
    cosine = jnp.where(((quarter + 1) & 2) == 2, -cosine, cosine)
    return sine, cosine


def forward(block, first_ref):
    rows = block.shape[1]
    high, low = split(block)
    return mm(jnp.concatenate([high, high], axis=1), first_ref[...]) + mm(low, first_ref[:rows, :])


def inverse(real, imag, inverse_ref):
    rows = real.shape[1]
    high, low = split(jnp.concatenate([real, imag], axis=1))
    both = mm(high, inverse_ref[...])
    return both[:, :rows] + both[:, rows:] + mm(low, inverse_ref[:, :rows])


def window_block(rates, start, rows, length):
    place = (lax.broadcasted_iota(jnp.int32, (1, rows), 1) + start).astype(F32) * (-1.0 / length)
    return jnp.exp(rates * place) * (1.0 / math.sqrt(length))


def prepare(w_one, w_two, w_three, b_one, b_two, order):
    one = jnp.concatenate(split(w_one.T), axis=0)
    two = jnp.concatenate(split(w_two.T), axis=0)
    three = jnp.concatenate(split(w_three.T), axis=0)
    col_one = jnp.broadcast_to(b_one, (order, order)).T
    col_two = jnp.broadcast_to(b_two, (order, order)).T
    return one, two, three, col_one, col_two


def network(feat_high, feat_low, one, two, col_one, col_two):
    count = feat_high.shape[1] // LANES
    act_one, cos_one = sin_cos(
        left_mm(one, feat_high, feat_low) + jnp.concatenate([col_one] * count, axis=1)
    )
    one_high, one_low = split(act_one)
    act_two, cos_two = sin_cos(
        left_mm(two, one_high, one_low) + jnp.concatenate([col_two] * count, axis=1)
    )
    two_high, two_low = split(act_two)
    return one_high, one_low, cos_one, two_high, two_low, cos_two


def lookup_table(embed, taps, pick):
    chosen = mm(pick, embed)
    channels = taps.shape[2]
    pieces = []
    for branch in range(3):
        part = chosen[:, branch * channels : (branch + 1) * channels]
        scaled = [
            part[tap * GROUP : (tap + 1) * GROUP] * taps[branch, tap : tap + 1, :]
            for tap in range(3)
        ]
        high = jnp.concatenate(scaled, axis=0)
        rounded = high.astype(BF16).astype(F32)
        rest = jnp.zeros((LANES - 6 * GROUP, channels), F32)
        pieces.append(jnp.concatenate([rounded, high - rounded, rest], axis=0).T)
    return jnp.concatenate(pieces, axis=0).astype(BF16)


def one_hot(tok_ref, block, code):
    rows = tok_ref.shape[1]

    def row(j):
        got = tok_ref[pl.ds(jnp.maximum(j, 0), 1), :]
        return jnp.where(j >= 0, got, 0)

    now = jnp.broadcast_to(row(block), (8, rows))
    before = jnp.broadcast_to(row(block - 1), (8, rows))
    lane = lax.broadcasted_iota(jnp.int32, (8, rows), 1)
    shifted = [now]
    for tap in (1, 2):
        shifted.append(
            jnp.where(lane < tap, pltpu.roll(before, tap, 1), pltpu.roll(now, tap, 1))
        )
    wide = [jnp.concatenate([s, s], axis=0) for s in shifted]
    rest = jnp.zeros((LANES - 6 * GROUP, rows), jnp.int32)
    spread = jnp.concatenate(wide + wide + [rest], axis=0)
    return jnp.where(spread == code, 1.0, 0.0).astype(BF16)


def pre_kernel(
    length, apart, *refs
):
    (embed, taps, pick, rates, skip, cot, w_one, b_one, w_two, b_two, w_three) = refs[:11]
    refs = refs[11:]
    if not apart:
        feat_high, feat_low, first = refs[:3]
        refs = refs[3:]
    table, rates_col, skip_col, cot_t = refs[:4]
    channels = cot.shape[1]
    table[...] = lookup_table(embed[...], taps[...], pick[...])
    rates_col[...] = jnp.broadcast_to(rates[...], (LANES, channels)).T
    skip_col[...] = jnp.broadcast_to(skip[...], (LANES, channels)).T
    cot_t[...] = cot[...].astype(F32).T
    if not apart:
        one_high, one_low, cos_one, two_high, two_low, cos_two, spectra = refs[4:]
        order = w_one.shape[1]
        one, two, three, col_one, col_two = prepare(
            w_one[...], w_two[...], w_three[...], b_one[...], b_two[...], order
        )
        made = network(feat_high[...], feat_low[...], one, two, col_one, col_two)
        for ref, value in zip((one_high, one_low, cos_one, two_high, two_low, cos_two), made):
            ref[...] = value
        for k in range(length // LANES):
            at = slice(k * LANES, (k + 1) * LANES)
            filt = left_mm(three, two_high[:, at], two_low[:, at]) * window_block(
                rates_col[...], k * LANES, LANES, length
            )
            spectra[k] = forward(filt, first)


def main_kernel(length, apart, *refs):
    (place, tok, code, first, inv, sign, table, rates_col, cot_t) = refs[:9]
    (w_two, w_three, feat_high, feat_low) = refs[9:13]
    refs = refs[13:]
    if apart:
        w_one, b_one, b_two = refs[:3]
        refs = refs[3:]
    else:
        one_high, one_low, cos_one, two_high, two_low, cos_two, spectra = refs[:7]
        refs = refs[7:]
    keep, send, mixed, query_t, signal_t = refs[:5]
    hot, spec, slope_high, slope_low, packed = refs[5:10]
    blocks, rows = tok.shape
    channels = cot_t.shape[0]
    order = w_two.shape[0]
    count = min(blocks, CHUNK)
    chunks = blocks // count
    own = place[0]
    bit = place[1]
    codes = code[...]
    signs = jnp.broadcast_to(sign[0:1, :], (channels, rows))

    three_split = split(w_three[...])
    three_stack = jnp.concatenate(three_split, axis=0)
    two_stack = jnp.concatenate(split(w_two[...]), axis=0)
    if apart:
        one_t, two_t, three_t, col_one, col_two = prepare(
            w_one[...], w_two[...], w_three[...], b_one[...], b_two[...], order
        )

    own_hot = one_hot(tok, own, codes)
    query = mm(table[:channels, :], own_hot)
    query_t[...] = query
    up = forward(cot_t[...] * query, first)
    up_real, up_imag = up[:, :rows], up[:, rows:]
    packed[...] = jnp.zeros(packed.shape, F32)

    def chunk(base):
        static = isinstance(base, int)
        slots = count if static else count + 1
        lane0 = base * rows if static else pl.multiple_of(base * rows, rows * count)
        for i in range(slots):
            hot[:, i * rows : (i + 1) * rows] = one_hot(tok, own - base - i, codes)
        span = pl.ds(lane0, count * rows)
        if apart:
            act_one_high, act_one_low, cosine_one, act_two_high, act_two_low, cosine_two = network(
                feat_high[:, span], feat_low[:, span], one_t, two_t, col_one, col_two
            )
        else:
            act_one_high, act_one_low, cosine_one, act_two_high, act_two_low, cosine_two = (
                r[:, span] for r in (one_high, one_low, cos_one, two_high, two_low, cos_two)
            )
        for i in range(slots):
            both = mm(table[channels:, :], hot[:, i * rows : (i + 1) * rows])
            signal = both[:channels] * both[channels:]
            if i == 0:
                if static:
                    signal_t[...] = signal
                else:

                    @pl.when(base == 0)
                    def _():
                        signal_t[...] = signal

            spec[i] = forward(signal, first)
        for i in range(count):
            real, imag = spec[i, :, :rows], spec[i, :, rows:]
            if i + 1 < slots:
                real = real - signs * spec[i + 1, :, rows:]
                imag = imag + signs * spec[i + 1, :, :rows]
            weight = window_block(rates_col[...], lane0 + i * rows, rows, length)
            if apart:
                at = slice(i * rows, (i + 1) * rows)
                filt = left_mm(three_t, act_two_high[:, at], act_two_low[:, at]) * weight
                got = forward(filt, first)
            else:
                got = spectra[base + i]
            g_real, g_imag = got[:, :rows], got[:, rows:]
            add_real = g_real * real - g_imag * imag
            add_imag = g_real * imag + g_imag * real
            if static and i == 0:
                mixed[:, :rows] = add_real
                mixed[:, rows:] = add_imag
            else:
                mixed[:, :rows] += add_real
                mixed[:, rows:] += add_imag
            lag = inverse(
                up_real * real + up_imag * imag, up_imag * real - up_real * imag, inv
            )
            high, low = split(lag * weight)
            slope_high[:, i * rows : (i + 1) * rows] = high
            slope_low[:, i * rows : (i + 1) * rows] = low

        slopes_high, slopes_low = slope_high[...], slope_low[...]
        grad_three = left_mm(
            jnp.concatenate([act_two_high, act_two_low], axis=0), slopes_high, slopes_low, cb=1
        )
        for slab in range(channels // LANES):
            packed[slab * order : (slab + 1) * order, :] += grad_three[
                :, slab * LANES : (slab + 1) * LANES
            ]
        back_two = left_mm(three_stack, slopes_high, slopes_low) * cosine_two
        two_back = split(back_two)
        grad_two = left_mm(
            jnp.concatenate([act_one_high, act_one_low], axis=0), *two_back, cb=1
        )
        back_one = left_mm(two_stack, *two_back) * cosine_one
        one_back = split(back_one)
        grad_one = left_mm(
            jnp.concatenate([feat_high[:, span], feat_low[:, span]], axis=0), *one_back, cb=1
        )
        ones = jnp.ones((8, count * rows), BF16)
        bias_one = mm(ones, one_back[0], cb=1) + mm(ones, one_back[1], cb=1)
        bias_two = mm(ones, two_back[0], cb=1) + mm(ones, two_back[1], cb=1)
        at = channels // LANES * order
        features = feat_high.shape[0]
        packed[at : at + features, :] += grad_one
        packed[at + features : at + features + order, :] += grad_two
        at = at + features + order
        packed[at : at + 8, :] += bias_one
        packed[at + 8 : at + 16, :] += bias_two

    if chunks == 1:
        chunk(0)
    else:
        mixed[...] = jnp.zeros(mixed.shape, F32)

        @pl.loop(0, chunks)
        def _(q):
            chunk(q * count)

    half = keep.shape[0]
    keep[...] = packed[pl.ds(pl.multiple_of(bit * half, 8), half), :]
    send[...] = packed[pl.ds(pl.multiple_of((1 - bit) * half, 8), half), :]


def gate_kernel(mixed, inv, query_t, signal_t, skip_col, out):
    rows = query_t.shape[1]
    convolved = inverse(mixed[:, :rows], mixed[:, rows:], inv)
    gated = query_t[...] * (convolved + skip_col[...] * signal_t[...])
    out[...] = gated.T.astype(BF16)


def unpack_kernel(place, mine, other, grad_one, bias_one, grad_two, bias_two, grad_three, whole):
    half = mine.shape[0]
    bit = place[1]
    whole[pl.ds(pl.multiple_of(bit * half, 8), half), :] = mine[...]
    whole[pl.ds(pl.multiple_of((1 - bit) * half, 8), half), :] = other[...]
    order = grad_three.shape[0]
    slabs = grad_three.shape[1] // LANES
    for slab in range(slabs):
        grad_three[:, slab * LANES : (slab + 1) * LANES] = whole[
            slab * order : (slab + 1) * order, :
        ]
    at = slabs * order
    features = grad_one.shape[0]
    grad_one[...] = whole[at : at + features, :]
    grad_two[...] = whole[at + features : at + features + order, :]
    at = at + features + order
    bias_one[...] = whole[at : at + 1, :]
    bias_two[...] = whole[at + 8 : at + 9, :]


def run(kernel, ins, outs, scratch=(), flops=0, smem=()):
    in_specs = [
        pl.BlockSpec(memory_space=pltpu.SMEM if i in smem else pltpu.VMEM) for i in range(len(ins))
    ]
    moved = sum(math.prod(a.shape) * a.dtype.itemsize for a in list(ins) + list(outs))
    return pl.pallas_call(
        kernel,
        out_shape=tuple(outs),
        in_specs=in_specs,
        out_specs=tuple(pl.BlockSpec(memory_space=pltpu.VMEM) for _ in outs),
        scratch_shapes=list(scratch),
        compiler_params=pltpu.CompilerParams(vmem_limit_bytes=VMEM),
        cost_estimate=pl.CostEstimate(flops=flops, bytes_accessed=moved, transcendentals=0),
    )(*ins)


def swap_with(block, axis, distance):
    size = lax.axis_size(axis)
    return lax.ppermute(block, axis, [(i, i ^ distance) for i in range(size)])


def all_added(block):
    steps = [("dp", 1 << i) for i in range(1, lax.axis_size("dp").bit_length() - 1)]
    steps += [("seq", 1 << i) for i in range(lax.axis_size("seq").bit_length() - 1)]
    cut = (block.shape[0] // 2 + 7) // 8 * 8
    parts = [block[:cut], block[cut:]]
    turn = len(steps) // 2
    for s in range(len(steps)):
        moves = (steps[s], steps[(s + turn) % len(steps)])
        parts = [part + swap_with(part, *move) for part, move in zip(parts, moves)]
    return jnp.concatenate(parts, axis=0)


def body(tokens, embed, taps, skip, rates, w_one, b_one, w_two, b_two, w_three, cotangent):
    blocks = lax.axis_size("seq")
    own = lax.axis_index("seq")
    bit = lax.axis_index("dp") % 2
    rows = tokens.shape[1]
    channels = skip.shape[0]
    features, order = w_one.shape
    length = rows * blocks
    apart = blocks > CHUNK
    shape = jax.ShapeDtypeStruct
    place = jnp.stack([own, bit]).astype(jnp.int32)

    gathered = lax.all_to_all(
        jnp.broadcast_to(tokens, (blocks, rows)), "seq", split_axis=0, concat_axis=0, tiled=True
    )

    feat_high, feat_low = (jnp.asarray(t) for t in feature_tables(length, features // 2))
    first, inv, sign = (jnp.asarray(t) for t in transform_tables(rows))
    code, pick = (jnp.asarray(t) for t in letter_tables(LANES))
    wide = (order, length)
    bias_rows = (b_one.reshape(1, order), b_two.reshape(1, order))
    pre_ins = [
        embed[:LANES], taps, pick, rates.reshape(1, channels), skip.reshape(1, channels),
        cotangent[0], w_one, bias_rows[0], w_two, bias_rows[1], w_three,
    ]
    pre_outs = [shape((3 * channels, LANES), BF16)] + [shape((channels, LANES), F32)] * 3
    if not apart:
        pre_ins += [feat_high, feat_low, first]
        pre_outs += [shape(wide, BF16), shape(wide, BF16), shape(wide, F32)] * 2
        pre_outs += [shape((blocks, channels, 2 * rows), F32)]
    table, rates_col, skip_col, cot_t, *made = run(
        functools.partial(pre_kernel, length, apart), pre_ins, pre_outs, flops=2 * 10**9
    )

    total = channels // LANES * order + features + order + 16
    half = (total // 2 + 7) // 8 * 8
    count = min(blocks, CHUNK)
    slots = count if blocks == count else count + 1
    main_ins = [place, gathered, code, first, inv, sign, table, rates_col, cot_t]
    main_ins += [w_two, w_three, feat_high, feat_low]
    main_ins += [w_one, *bias_rows] if apart else made
    keep, send, mixed, query_t, signal_t = run(
        functools.partial(main_kernel, length, apart),
        main_ins,
        [shape((half, LANES), F32)] * 2
        + [shape((channels, 2 * rows), F32)]
        + [shape((channels, rows), F32)] * 2,
        scratch=[
            pltpu.VMEM((LANES, slots * rows), BF16),
            pltpu.VMEM((slots, channels, 2 * rows), F32),
            pltpu.VMEM((channels, count * rows), BF16),
            pltpu.VMEM((channels, count * rows), BF16),
            pltpu.VMEM((2 * half, LANES), F32),
        ],
        flops=6 * 10**9,
        smem=(0,),
    )
    summed = all_added(keep + swap_with(send, "dp", 1))
    (gated,) = run(
        gate_kernel,
        [mixed, inv, query_t, signal_t, skip_col],
        [shape((rows, channels), BF16)],
        flops=3 * 10**8,
    )
    other = swap_with(summed, "dp", 1)
    grad_one, bias_one, grad_two, bias_two, grad_three = run(
        unpack_kernel,
        [place, summed, other],
        [
            shape((features, order), F32), shape((1, order), F32), shape((order, order), F32),
            shape((1, order), F32), shape((order, channels), F32),
        ],
        scratch=[pltpu.VMEM((2 * half, LANES), F32)],
        smem=(0,),
    )
    return (
        gated[None], grad_one, bias_one.reshape(order), grad_two, bias_two.reshape(order),
        grad_three,
    )


def solution(mesh):
    return jax.shard_map(
        body,
        mesh=mesh,
        in_specs=(
            P("dp", "seq"),
            P(),
            P(),
            P(),
            P(),
            P(),
            P(),
            P(),
            P(),
            P(),
            P("dp", "seq", None),
        ),
        out_specs=(P("dp", "seq", None), P(), P(), P(), P(), P()),
        check_vma=False,
    )
```

time: 358 us -> 61.6 us (0.17)
  waiting for transfers between devices: 195 us -> 9 us
  blocking collectives: 40.9 us -> 0 us
  matrix products: 34.8 us -> 0 us
  Pallas kernels: 0 us -> 22.7 us
  starting transfers between devices: 38.3 us -> 22.8 us
  local copies, waits for them, and re-layouts: 19.7 us -> 4.35 us
  between operations: 14.5 us -> 0.72 us
  other arithmetic: 12.6 us -> 1.69 us
    all_to_all x8 -> x1, waiting for transfers between devices: 104 us -> 0.01 us  [body(): lax.all_to_all(jnp.broadcast_to(tokens, (blocks, rows)), 'seq', split_axi...]
    psum x1 -> x0, waiting for transfers between devices: 91.6 us -> none  [body(): lax.psum((grad_one, bias_one, grad_two, bias_two, grad_three), ('seq', 'd...]
    psum x1 -> x0, blocking collectives: 40.9 us -> none  [body(): lax.psum((grad_one, bias_one, grad_two, bias_two, grad_three), ('seq', 'd...]
    dot_general x21 -> x0, matrix products: 34.8 us -> none  [the longest x8 8.81 us: matmul(): jnp.dot(left, right, precision=precise, preferred_element_type=jnp.float32)]
    all_to_all x8 -> x1, starting transfers between devices: 33.2 us -> 7.28 us  [body(): lax.all_to_all(jnp.broadcast_to(tokens, (blocks, rows)), 'seq', split_axi...]
    pallas_call x0 -> x4, Pallas kernels: none -> 22.7 us  [run(): pl.pallas_call(kernel, out_shape=tuple(outs), in_specs=in_specs, out_spec...]
    ppermute x1 -> x10, starting transfers between devices: 4.86 us -> 15.6 us  [swap_with(): return lax.ppermute(block, axis, [(i, i ^ distance) for i in range(size)])]
    reshape x4 -> x0, local copies, waits for them, and re-layouts: 10.7 us -> none  [forward_transform(): mixture.reshape(seq_count, 2, devices, 2, per_slot, chan_count)]
  transfers between devices with their start and end apart: 11 -> 11, of which waited for: 8 -> 6; matrix products, arithmetic and copies ran while one was open for 15% -> 4% of each run, Pallas kernels for 0% -> 17%
where the time goes in v1:
time: 61.6 us; the launch traced here: 61.3 us
  starting transfers between devices  22.8 us (37%)
  Pallas kernels  22.7 us (37%)
  waiting for transfers between devices  9 us (15%)
  local copies, waits for them, and re-layouts  4.35 us (7%)
  other arithmetic  1.69 us (3%)
  between operations  0.72 us (1%)
    pallas_call x4, Pallas kernels, run(): pl.pallas_call(kernel, out_shape=tuple(outs), in_specs=in_specs, out_spec...  22.7 us
    ppermute x10, starting transfers between devices, swap_with(): return lax.ppermute(block, axis, [(i, i ^ distance) for i in range(size)])  15.6 us
    ppermute x10, waiting for transfers between devices, swap_with(): return lax.ppermute(block, axis, [(i, i ^ distance) for i in range(size)])  9 us
    all_to_all x1, starting transfers between devices, body(): lax.all_to_all(jnp.broadcast_to(tokens, (blocks, rows)), 'seq', split_axi...  7.28 us
    slice x1, local copies, waits for them, and re-layouts, body(): embed[:LANES]  1.8 us
    unnamed x6, local copies, waits for them, and re-layouts  1.28 us
    broadcast_in_dim x1, local copies, waits for them, and re-layouts, body(): jnp.broadcast_to(tokens, (blocks, rows))  1.25 us
  transfers between devices with their start and end apart: 11, of which 6 were waited for; matrix products, arithmetic and copies ran while one was open for 4% of the time, Pallas kernels for 17%

profile of v1, /device:TPU:0, one launch (start us, length us, event | category | flops | bytes accessed | tf_op | source)
XLA Modules:
  0.0 61.3 jit_solution(16580950647993453571)
XLA Ops:
  0.6 1.2 %broadcast_in_dim.8 = s32[8,1,128]{2,1,0:T(1,128)} broadcast(s32[128]{0:T(128)} %bitcast.14), dimensions={2} | broadcast | bytes 4608 | tf_op jit(solution)/shard_map/broadcast_in_dim | solution.py:419
  1.9 7.3 %all-to-all-start = ((s32[8,1,128]{2,1,0:T(1,128)}), s32[8,1,128]{2,1,0:T(1,128)S(1)}, u32[]{:S(2)}, u32[]{:S(2)}) async-start(s32[8,1,128]{2,1,0:T(1,128)} %broadcast_in_dim.8), calls=%async_computation | async-start | bytes 8192 | tf_op jit(solution)/shard_map/all_to_all | solution.py:418
  9.2 1.8 %slice.9.refs_0_ = bf16[128,1536]{1,0:T(8,128)(2,1)} slice(bf16[512,1536]{1,0:T(8,128)(2,1)} %param.19), slice={[0:128], [0:1536]} | slice | bytes 786432 | tf_op jit(solution)/shard_map/slice | solution.py:428
  11.0 7.9 %shard_map.220 = (bf16[1536,128]{1,0:T(8,128)(2,1)}, f32[512,128]{1,0:T(8,128)}, f32[512,128]{1,0:T(8,128)}, f32[512,128]{1,0:T(8,128)}, bf16[128,1024]{1,0:T(8,...) custom-call(bf16[128,1536]{1,0:T(8,128)(2,1)} %slice.9.refs_0_, ...), custom_call_target="tpu_custom_call" | custom-call | flops 2000000000 | bytes 9100288 | tf_op jit(solution)/shard_map/pallas_call | solution.py:378
  18.9 0.6 pad_add_fusion.refs_0_.place
  19.5 0.6 copy-done.2
  20.1 10.5 %shard_map.221 = (f32[392,128]{1,0:T(8,128)}, f32[392,128]{1,0:T(8,128)}, f32[512,256]{1,0:T(8,128)}, f32[512,128]{1,0:T(8,128)}, f32[512,128]{1,0:T(8,128)}) custom-call(s32[2]{0:T(128)} %pad_add_fusion.refs_0_.place, s32[8,128]{1,0:T(8,128)} %bitcast.13, s32[128,128]{1,0:T(8,128)} %constant.41.clone.refs_2_, ...), custom_call_target="tpu_custom_call" | custom-call | flops 6000000000 | bytes 9846792 | tf_op jit(solution)/shard_map/pallas_call | solution.py:378
  30.7 1.6 %collective-permute-done = f32[392,128]{1,0:T(8,128)S(1)} collective-permute-done((f32[392,128]{1,0:T(8,128)}, f32[392,128]{1,0:T(8,128)S(1)}, u32[]{:S(2)}, u32[]{:S(2)}) %collective-permute-start) | collective-permute-done | bytes 200736 | tf_op jit(solution)/shard_map/ppermute | solution.py:391
  32.4 1.0 %add.32 = f32[392,128]{1,0:T(8,128)S(1)} add(f32[392,128]{1,0:T(8,128)} %get-tuple-element.41, f32[392,128]{1,0:T(8,128)S(1)} %collective-permute-done) | non-fusion elementwise | flops 50176 | bytes 602112 | tf_op jit(solution)/shard_map/add | solution.py:463
  33.3 1.6 %collective-permute-start.1 = (f32[200,128]{1,0:T(8,128)S(1)}, f32[200,128]{1,0:T(8,128)S(1)}, u32[]{:S(2)}, u32[]{:S(2)}) collective-permute-start(f32[200,128]{1,0:T(8,128)S(1)} %slice.12), channel_id=1, source_target_pairs={{0,2},{1,3},{2,0},{3,1},{4,6},{5,7},{6,4},{7,5},{8,10},{9,11},{10,... | collective-permute-start | bytes 307208 | tf_op jit(solution)/shard_map/ppermute | solution.py:391
  34.9 2.1 %collective-permute-start.5 = (f32[192,128]{1,0:T(8,128)S(1)}, f32[192,128]{1,0:T(8,128)S(1)}, u32[]{:S(2)}, u32[]{:S(2)}) collective-permute-start(f32[192,128]{1,0:T(8,128)S(1)} %slice.13), channel_id=1, source_target_pairs={{0,8},{4,12},{8,0},{12,4},{16,24},{20,28},{24,16},{28,20},{1,9},{5... | collective-permute-start | bytes 294920 | tf_op jit(solution)/shard_map/ppermute | solution.py:391
  37.0 1.3 %collective-permute-done.1 = f32[200,128]{1,0:T(8,128)S(1)} collective-permute-done((f32[200,128]{1,0:T(8,128)S(1)}, f32[200,128]{1,0:T(8,128)S(1)}, u32[]{:S(2)}, u32[]{:S(2)}) %collective-permute-start.1) | collective-permute-done | bytes 102432 | tf_op jit(solution)/shard_map/ppermute | solution.py:391
  38.3 2.1 %collective-permute-start.2 = (f32[200,128]{1,0:T(8,128)S(1)}, f32[200,128]{1,0:T(8,128)S(1)}, u32[]{:S(2)}, u32[]{:S(2)}) collective-permute-start(f32[200,128]{1,0:T(8,128)S(1)} %slice_add_fusion.1), channel_id=1, source_target_pairs={{0,4},{4,0},{8,12},{12,8},{16,20},{20,16},{24,28},{28,24},{1,5},{5... | collective-permute-start | bytes 307208 | tf_op jit(solution)/shard_map/ppermute | solution.py:391
  40.4 2.4 %collective-permute-start.6 = (f32[192,128]{1,0:T(8,128)S(1)}, f32[192,128]{1,0:T(8,128)S(1)}, u32[]{:S(2)}, u32[]{:S(2)}) collective-permute-start(f32[192,128]{1,0:T(8,128)S(1)} %slice_add_fusion), channel_id=1, source_target_pairs={{0,16},{4,20},{8,24},{12,28},{16,0},{20,4},{24,8},{28,12},{1,17},{... | collective-permute-start | bytes 294920 | tf_op jit(solution)/shard_map/ppermute | solution.py:391
  43.1 2.1 %collective-permute-start.3 = (f32[200,128]{1,0:T(8,128)S(1)}, f32[200,128]{1,0:T(8,128)S(1)}, u32[]{:S(2)}, u32[]{:S(2)}) collective-permute-start(f32[200,128]{1,0:T(8,128)S(1)} %add.34), channel_id=1, source_target_pairs={{0,8},{4,12},{8,0},{12,4},{16,24},{20,28},{24,16},{28,20},{1,9},{5... | collective-permute-start | bytes 307208 | tf_op jit(solution)/shard_map/ppermute | solution.py:391
  45.2 1.7 %collective-permute-done.6 = f32[192,128]{1,0:T(8,128)S(1)} collective-permute-done((f32[192,128]{1,0:T(8,128)S(1)}, f32[192,128]{1,0:T(8,128)S(1)}, u32[]{:S(2)}, u32[]{:S(2)}) %collective-permute-start.6) | collective-permute-done | bytes 98336 | tf_op jit(solution)/shard_map/ppermute | solution.py:391
  46.8 1.5 %collective-permute-start.7 = (f32[192,128]{1,0:T(8,128)S(1)}, f32[192,128]{1,0:T(8,128)S(1)}, u32[]{:S(2)}, u32[]{:S(2)}) collective-permute-start(f32[192,128]{1,0:T(8,128)S(1)} %add.38), channel_id=1, source_target_pairs={{0,2},{1,3},{2,0},{3,1},{4,6},{5,7},{6,4},{7,5},{8,10},{9,11},{10,... | collective-permute-start | bytes 294920 | tf_op jit(solution)/shard_map/ppermute | solution.py:391
  48.4 2.4 %collective-permute-start.4 = (f32[200,128]{1,0:T(8,128)S(1)}, f32[200,128]{1,0:T(8,128)S(1)}, u32[]{:S(2)}, u32[]{:S(2)}) collective-permute-start(f32[200,128]{1,0:T(8,128)S(1)} %add.35), channel_id=1, source_target_pairs={{0,16},{4,20},{8,24},{12,28},{16,0},{20,4},{24,8},{28,12},{1,17},{... | collective-permute-start | bytes 307208 | tf_op jit(solution)/shard_map/ppermute | solution.py:391
  50.8 0.7 %collective-permute-done.7 = f32[192,128]{1,0:T(8,128)S(1)} collective-permute-done((f32[192,128]{1,0:T(8,128)S(1)}, f32[192,128]{1,0:T(8,128)S(1)}, u32[]{:S(2)}, u32[]{:S(2)}) %collective-permute-start.7) | collective-permute-done | bytes 98336 | tf_op jit(solution)/shard_map/ppermute | solution.py:391
  51.5 1.2 %collective-permute-start.8 = (f32[192,128]{1,0:T(8,128)S(1)}, f32[192,128]{1,0:T(8,128)S(1)}, u32[]{:S(2)}, u32[]{:S(2)}) collective-permute-start(f32[192,128]{1,0:T(8,128)S(1)} %add.39), channel_id=1, source_target_pairs={{0,4},{4,0},{8,12},{12,8},{16,20},{20,16},{24,28},{28,24},{1,5},{5... | collective-permute-start | bytes 294920 | tf_op jit(solution)/shard_map/ppermute | solution.py:391
  52.8 3.5 %collective-permute-done.8 = f32[192,128]{1,0:T(8,128)S(1)} collective-permute-done((f32[192,128]{1,0:T(8,128)S(1)}, f32[192,128]{1,0:T(8,128)S(1)}, u32[]{:S(2)}, u32[]{:S(2)}) %collective-permute-start.8) | collective-permute-done | bytes 98336 | tf_op jit(solution)/shard_map/ppermute | solution.py:391
  56.4 2.4 %shard_map.222 = bf16[128,512]{1,0:T(8,128)(2,1)} custom-call(f32[512,256]{1,0:T(8,128)} %get-tuple-element.37.mixed, bf16[256,256]{1,0:T(8,128)(2,1)} %constant.39.clone.refs_4_.inv, f32[512,128]{1,0:T(8,128)} %get-tuple-element.38.query_t, f32[512,128]{1,0:T(8,128)} %get-tuple-element.39.signal_t, f32[512,128]{1,0:T(8,128)} %get-tuple-element.40.skip_col), custom_call_target="tpu_custom_call" | custom-call | flops 300000000 | bytes 1572864 | tf_op jit(solution)/shard_map/pallas_call | solution.py:378
  58.8 0.7 %copy-done.1 = f32[392,128]{1,0:T(8,128)} copy-done((f32[392,128]{1,0:T(8,128)}, f32[392,128]{1,0:T(8,128)S(1)}, u32[]{:S(2)}) %copy-start.1) | copy-done | bytes 200728
  59.5 1.8 %shard_map.223 = (f32[128,128]{1,0:T(8,128)}, f32[1,128]{1,0:T(1,128)}, f32[128,128]{1,0:T(8,128)}, f32[1,128]{1,0:T(1,128)}, f32[128,512]{1,0:T(8,128)}) custom-call(s32[2]{0:T(128)} %pad_add_fusion.refs_0_.place, f32[392,128]{1,0:T(8,128)} %copy-done, f32[392,128]{1,0:T(8,128)} %copy-done.1), custom_call_target="tpu_custom_call" | custom-call | bytes 795656 | tf_op jit(solution)/shard_map/pallas_call | solution.py:378
  (23 shorter events, 0.5 us)
Async XLA Ops:
  1.9 17.6 %all-to-all-start = ((s32[8,1,128]{2,1,0:T(1,128)}), s32[8,1,128]{2,1,0:T(1,128)S(1)}, u32[]{:S(2)}, u32[]{:S(2)}) async-start(s32[8,1,128]{2,1,0:T(1,128)} %broadcast_in_dim.8), calls=%async_computation | async-start | bytes 8192 | tf_op jit(solution)/shard_map/all_to_all | solution.py:418
  19.5 0.6 copy-start.2
  30.6 1.7 %collective-permute-start = (f32[392,128]{1,0:T(8,128)}, f32[392,128]{1,0:T(8,128)S(1)}, u32[]{:S(2)}, u32[]{:S(2)}) collective-permute-start(f32[392,128]{1,0:T(8,128)} %get-tuple-element.42), channel_id=1, source_target_pairs={{0,1},{1,0},{2,3},{3,2},{4,5},{5,4},{6,7},{7,6},{8,9},{9,8},{10,11... | collective-permute-start | bytes 602120 | tf_op jit(solution)/shard_map/ppermute | solution.py:391
  33.3 5.0 %collective-permute-start.1 = (f32[200,128]{1,0:T(8,128)S(1)}, f32[200,128]{1,0:T(8,128)S(1)}, u32[]{:S(2)}, u32[]{:S(2)}) collective-permute-start(f32[200,128]{1,0:T(8,128)S(1)} %slice.12), channel_id=1, source_target_pairs={{0,2},{1,3},{2,0},{3,1},{4,6},{5,7},{6,4},{7,5},{8,10},{9,11},{10,... | collective-permute-start | bytes 307208 | tf_op jit(solution)/shard_map/ppermute | solution.py:391
  34.9 5.5 %collective-permute-start.5 = (f32[192,128]{1,0:T(8,128)S(1)}, f32[192,128]{1,0:T(8,128)S(1)}, u32[]{:S(2)}, u32[]{:S(2)}) collective-permute-start(f32[192,128]{1,0:T(8,128)S(1)} %slice.13), channel_id=1, source_target_pairs={{0,8},{4,12},{8,0},{12,4},{16,24},{20,28},{24,16},{28,20},{1,9},{5... | collective-permute-start | bytes 294920 | tf_op jit(solution)/shard_map/ppermute | solution.py:391
  38.3 4.7 %collective-permute-start.2 = (f32[200,128]{1,0:T(8,128)S(1)}, f32[200,128]{1,0:T(8,128)S(1)}, u32[]{:S(2)}, u32[]{:S(2)}) collective-permute-start(f32[200,128]{1,0:T(8,128)S(1)} %slice_add_fusion.1), channel_id=1, source_target_pairs={{0,4},{4,0},{8,12},{12,8},{16,20},{20,16},{24,28},{28,24},{1,5},{5... | collective-permute-start | bytes 307208 | tf_op jit(solution)/shard_map/ppermute | solution.py:391
  40.4 6.4 %collective-permute-start.6 = (f32[192,128]{1,0:T(8,128)S(1)}, f32[192,128]{1,0:T(8,128)S(1)}, u32[]{:S(2)}, u32[]{:S(2)}) collective-permute-start(f32[192,128]{1,0:T(8,128)S(1)} %slice_add_fusion), channel_id=1, source_target_pairs={{0,16},{4,20},{8,24},{12,28},{16,0},{20,4},{24,8},{28,12},{1,17},{... | collective-permute-start | bytes 294920 | tf_op jit(solution)/shard_map/ppermute | solution.py:391
  43.1 5.3 %collective-permute-start.3 = (f32[200,128]{1,0:T(8,128)S(1)}, f32[200,128]{1,0:T(8,128)S(1)}, u32[]{:S(2)}, u32[]{:S(2)}) collective-permute-start(f32[200,128]{1,0:T(8,128)S(1)} %add.34), channel_id=1, source_target_pairs={{0,8},{4,12},{8,0},{12,4},{16,24},{20,28},{24,16},{28,20},{1,9},{5... | collective-permute-start | bytes 307208 | tf_op jit(solution)/shard_map/ppermute | solution.py:391
  46.8 4.7 %collective-permute-start.7 = (f32[192,128]{1,0:T(8,128)S(1)}, f32[192,128]{1,0:T(8,128)S(1)}, u32[]{:S(2)}, u32[]{:S(2)}) collective-permute-start(f32[192,128]{1,0:T(8,128)S(1)} %add.38), channel_id=1, source_target_pairs={{0,2},{1,3},{2,0},{3,1},{4,6},{5,7},{6,4},{7,5},{8,10},{9,11},{10,... | collective-permute-start | bytes 294920 | tf_op jit(solution)/shard_map/ppermute | solution.py:391
  48.4 7.8 %collective-permute-start.4 = (f32[200,128]{1,0:T(8,128)S(1)}, f32[200,128]{1,0:T(8,128)S(1)}, u32[]{:S(2)}, u32[]{:S(2)}) collective-permute-start(f32[200,128]{1,0:T(8,128)S(1)} %add.35), channel_id=1, source_target_pairs={{0,16},{4,20},{8,24},{12,28},{16,0},{20,4},{24,8},{28,12},{1,17},{... | collective-permute-start | bytes 307208 | tf_op jit(solution)/shard_map/ppermute | solution.py:391
  51.5 4.7 %collective-permute-start.8 = (f32[192,128]{1,0:T(8,128)S(1)}, f32[192,128]{1,0:T(8,128)S(1)}, u32[]{:S(2)}, u32[]{:S(2)}) collective-permute-start(f32[192,128]{1,0:T(8,128)S(1)} %add.39), channel_id=1, source_target_pairs={{0,4},{4,0},{8,12},{12,8},{16,20},{20,16},{24,28},{28,24},{1,5},{5... | collective-permute-start | bytes 294920 | tf_op jit(solution)/shard_map/ppermute | solution.py:391
  56.3 2.5 %copy-start = (f32[392,128]{1,0:T(8,128)}, f32[392,128]{1,0:T(8,128)S(1)}, u32[]{:S(2)}) copy-start(f32[392,128]{1,0:T(8,128)S(1)} %pad_maximum_fusion.mine) | copy-start | bytes 602116
  56.3 2.5 %collective-permute-start.9 = (f32[392,128]{1,0:T(8,128)S(1)}, f32[392,128]{1,0:T(8,128)S(1)}, u32[]{:S(2)}, u32[]{:S(2)}) collective-permute-start(f32[392,128]{1,0:T(8,128)S(1)} %pad_maximum_fusion.mine), channel_id=1, source_target_pairs={{0,1},{1,0},{2,3},{3,2},{4,5},{5,4},{6,7},{7,6},{8,9},{9,8},{10,11... | collective-permute-start | bytes 602120 | tf_op jit(solution)/shard_map/ppermute | solution.py:391
  58.8 0.7 %copy-start.1 = (f32[392,128]{1,0:T(8,128)}, f32[392,128]{1,0:T(8,128)S(1)}, u32[]{:S(2)}) copy-start(f32[392,128]{1,0:T(8,128)S(1)} %collective-permute-done.9.other) | copy-start | bytes 602116

commit v2 on v1

--- a/solution.py
+++ b/solution.py
@@ -14,7 +14,8 @@
 GROUP = 16
 LANES = 128
 CHUNK = 8
-VMEM = 56 * 1024 * 1024
+SMALL = 24 * 1024 * 1024
+LARGE = 56 * 1024 * 1024
 F32 = jnp.float32
 BF16 = jnp.bfloat16
 
@@ -36,7 +37,7 @@
     numbers = np.array(band_numbers(length, band_count), np.int64)
     residue = (numbers[:, None] * np.arange(length, dtype=np.int64)[None, :]) % length
     angles = residue * (2.0 * math.pi / length)
-    return halves(np.concatenate([np.sin(angles), np.cos(angles)], axis=0))
+    return np.concatenate(halves(np.concatenate([np.sin(angles), np.cos(angles)], axis=0)), axis=0)
 
 
 @functools.cache
@@ -125,17 +126,18 @@
     return one, two, three, col_one, col_two
 
 
-def network(feat_high, feat_low, one, two, col_one, col_two):
-    count = feat_high.shape[1] // LANES
+def network(feat, one, two, col_one, col_two):
+    count = feat.shape[1] // LANES
+    size = feat.shape[0] // 2
     act_one, cos_one = sin_cos(
-        left_mm(one, feat_high, feat_low) + jnp.concatenate([col_one] * count, axis=1)
+        left_mm(one, feat[:size], feat[size:]) + jnp.concatenate([col_one] * count, axis=1)
     )
     one_high, one_low = split(act_one)
     act_two, cos_two = sin_cos(
         left_mm(two, one_high, one_low) + jnp.concatenate([col_two] * count, axis=1)
     )
-    two_high, two_low = split(act_two)
-    return one_high, one_low, cos_one, two_high, two_low, cos_two
+    act_one = jnp.concatenate([one_high, one_low], axis=0)
+    return act_one, cos_one, jnp.concatenate(split(act_two), axis=0), cos_two
 
 
 def lookup_table(embed, taps, pick):
@@ -155,11 +157,11 @@
     return jnp.concatenate(pieces, axis=0).astype(BF16)
 
 
-def one_hot(tok_ref, block, code):
+def one_hot(tok_ref, own, block, code):
     rows = tok_ref.shape[1]
 
     def row(j):
-        got = tok_ref[pl.ds(jnp.maximum(j, 0), 1), :]
+        got = tok_ref[pl.ds(jnp.maximum(j, 0) ^ own, 1), :]
         return jnp.where(j >= 0, got, 0)
 
     now = jnp.broadcast_to(row(block), (8, rows))
@@ -176,88 +178,78 @@
     return jnp.where(spread == code, 1.0, 0.0).astype(BF16)
 
 
-def pre_kernel(
-    length, apart, *refs
-):
-    (embed, taps, pick, rates, skip, cot, w_one, b_one, w_two, b_two, w_three) = refs[:11]
-    refs = refs[11:]
+def network_kernel(apart, w_one, b_one, w_two, b_two, w_three, feat, *outs):
+    two_back, three_back = outs[:2]
+    two_back[...] = jnp.concatenate(split(w_two[...]), axis=0)
+    three_back[...] = jnp.concatenate(split(w_three[...]), axis=0)
+    order = w_one.shape[1]
+    made = prepare(w_one[...], w_two[...], w_three[...], b_one[...], b_two[...], order)
     if not apart:
-        feat_high, feat_low, first = refs[:3]
-        refs = refs[3:]
-    table, rates_col, skip_col, cot_t = refs[:4]
+        one, two, three, col_one, col_two = made
+        made = (*network(feat[...], one, two, col_one, col_two), three)
+    for ref, value in zip(outs[2:], made):
+        ref[...] = value
+
+
+def filter_kernel(length, rates, act_two, three, first, rates_col, spectra):
+    channels = rates.shape[1]
+    order = act_two.shape[0] // 2
+    rates_col[...] = jnp.broadcast_to(rates[...], (LANES, channels)).T
+    for k in range(length // LANES):
+        at = slice(k * LANES, (k + 1) * LANES)
+        filt = left_mm(three[...], act_two[:order, at], act_two[order:, at])
+        filt = filt * window_block(rates_col[...], k * LANES, LANES, length)
+        spectra[k] = forward(filt, first)
+
+
+def table_kernel(embed_all, taps, pick, skip, rates, cot, table, skip_col, rates_col, cot_t, embed):
+    pltpu.sync_copy(embed_all.at[pl.ds(0, LANES), :], embed)
     channels = cot.shape[1]
     table[...] = lookup_table(embed[...], taps[...], pick[...])
+    skip_col[...] = jnp.broadcast_to(skip[...], (LANES, channels)).T
     rates_col[...] = jnp.broadcast_to(rates[...], (LANES, channels)).T
-    skip_col[...] = jnp.broadcast_to(skip[...], (LANES, channels)).T
     cot_t[...] = cot[...].astype(F32).T
-    if not apart:
-        one_high, one_low, cos_one, two_high, two_low, cos_two, spectra = refs[4:]
-        order = w_one.shape[1]
-        one, two, three, col_one, col_two = prepare(
-            w_one[...], w_two[...], w_three[...], b_one[...], b_two[...], order
-        )
-        made = network(feat_high[...], feat_low[...], one, two, col_one, col_two)
-        for ref, value in zip((one_high, one_low, cos_one, two_high, two_low, cos_two), made):
-            ref[...] = value
-        for k in range(length // LANES):
-            at = slice(k * LANES, (k + 1) * LANES)
-            filt = left_mm(three, two_high[:, at], two_low[:, at]) * window_block(
-                rates_col[...], k * LANES, LANES, length
-            )
-            spectra[k] = forward(filt, first)
 
 
 def main_kernel(length, apart, *refs):
-    (place, tok, code, first, inv, sign, table, rates_col, cot_t) = refs[:9]
-    (w_two, w_three, feat_high, feat_low) = refs[9:13]
-    refs = refs[13:]
+    tok = refs[0]
+    table, rates_col, cot_t, feat, first, inv, sign, code, two_back, three_back = refs[1:11]
     if apart:
-        w_one, b_one, b_two = refs[:3]
-        refs = refs[3:]
+        one_t, two_t, three_t, col_one, col_two = (r[...] for r in refs[11:16])
     else:
-        one_high, one_low, cos_one, two_high, two_low, cos_two, spectra = refs[:7]
-        refs = refs[7:]
-    keep, send, mixed, query_t, signal_t = refs[:5]
-    hot, spec, slope_high, slope_low, packed = refs[5:10]
+        one_all, cos_one, two_all, cos_two, spectra = refs[11:16]
+    keep, send, mixed, query_t, signal_t = refs[16:21]
+    hot, spec, slope_high, slope_low, packed = refs[21:26]
     blocks, rows = tok.shape
     channels = cot_t.shape[0]
-    order = w_two.shape[0]
+    order = two_back.shape[1]
     count = min(blocks, CHUNK)
     chunks = blocks // count
-    own = place[0]
-    bit = place[1]
+    own = lax.axis_index("seq")
+    bit = lax.axis_index("dp") % 2
     codes = code[...]
     signs = jnp.broadcast_to(sign[0:1, :], (channels, rows))
 
-    three_split = split(w_three[...])
-    three_stack = jnp.concatenate(three_split, axis=0)
-    two_stack = jnp.concatenate(split(w_two[...]), axis=0)
-    if apart:
-        one_t, two_t, three_t, col_one, col_two = prepare(
-            w_one[...], w_two[...], w_three[...], b_one[...], b_two[...], order
-        )
-
-    own_hot = one_hot(tok, own, codes)
+    own_hot = one_hot(tok, own, own, codes)
     query = mm(table[:channels, :], own_hot)
     query_t[...] = query
     up = forward(cot_t[...] * query, first)
     up_real, up_imag = up[:, :rows], up[:, rows:]
-    packed[...] = jnp.zeros(packed.shape, F32)
 
     def chunk(base):
         static = isinstance(base, int)
         slots = count if static else count + 1
         lane0 = base * rows if static else pl.multiple_of(base * rows, rows * count)
         for i in range(slots):
-            hot[:, i * rows : (i + 1) * rows] = one_hot(tok, own - base - i, codes)
+            hot[:, i * rows : (i + 1) * rows] = one_hot(tok, own, own - base - i, codes)
         span = pl.ds(lane0, count * rows)
         if apart:
-            act_one_high, act_one_low, cosine_one, act_two_high, act_two_low, cosine_two = network(
-                feat_high[:, span], feat_low[:, span], one_t, two_t, col_one, col_two
+            act_one, cosine_one, act_two, cosine_two = network(
+                feat[:, span], one_t, two_t, col_one, col_two
             )
         else:
-            act_one_high, act_one_low, cosine_one, act_two_high, act_two_low, cosine_two = (
-                r[:, span] for r in (one_high, one_low, cos_one, two_high, two_low, cos_two)
+            act_one, cosine_one, act_two, cosine_two = (
+                r[:, span] for r in (one_all, cos_one, two_all, cos_two)
             )
         for i in range(slots):
             both = mm(table[channels:, :], hot[:, i * rows : (i + 1) * rows])
@@ -280,7 +272,7 @@
             weight = window_block(rates_col[...], lane0 + i * rows, rows, length)
             if apart:
                 at = slice(i * rows, (i + 1) * rows)
-                filt = left_mm(three_t, act_two_high[:, at], act_two_low[:, at]) * weight
+                filt = left_mm(three_t, act_two[:order, at], act_two[order:, at]) * weight
                 got = forward(filt, first)
             else:
                 got = spectra[base + i]
@@ -300,39 +292,39 @@
             slope_high[:, i * rows : (i + 1) * rows] = high
             slope_low[:, i * rows : (i + 1) * rows] = low
 
+        def put(at, value):
+            if static:
+                packed[at : at + value.shape[0], :] = value
+            else:
+                packed[at : at + value.shape[0], :] += value
+
         slopes_high, slopes_low = slope_high[...], slope_low[...]
-        grad_three = left_mm(
-            jnp.concatenate([act_two_high, act_two_low], axis=0), slopes_high, slopes_low, cb=1
-        )
+        grad_three = left_mm(act_two, slopes_high, slopes_low, cb=1)
         for slab in range(channels // LANES):
-            packed[slab * order : (slab + 1) * order, :] += grad_three[
-                :, slab * LANES : (slab + 1) * LANES
-            ]
-        back_two = left_mm(three_stack, slopes_high, slopes_low) * cosine_two
-        two_back = split(back_two)
-        grad_two = left_mm(
-            jnp.concatenate([act_one_high, act_one_low], axis=0), *two_back, cb=1
-        )
-        back_one = left_mm(two_stack, *two_back) * cosine_one
-        one_back = split(back_one)
-        grad_one = left_mm(
-            jnp.concatenate([feat_high[:, span], feat_low[:, span]], axis=0), *one_back, cb=1
-        )
+            put(slab * order, grad_three[:, slab * LANES : (slab + 1) * LANES])
+        back_two = left_mm(three_back[...], slopes_high, slopes_low) * cosine_two
+        two_split = split(back_two)
+        back_one = left_mm(two_back[...], *two_split) * cosine_one
+        one_split = split(back_one)
+        grad_two = left_mm(act_one, *two_split, cb=1)
+        grad_one = left_mm(feat[:, span], *one_split, cb=1)
         ones = jnp.ones((8, count * rows), BF16)
-        bias_one = mm(ones, one_back[0], cb=1) + mm(ones, one_back[1], cb=1)
-        bias_two = mm(ones, two_back[0], cb=1) + mm(ones, two_back[1], cb=1)
         at = channels // LANES * order
-        features = feat_high.shape[0]
-        packed[at : at + features, :] += grad_one
-        packed[at + features : at + features + order, :] += grad_two
-        at = at + features + order
-        packed[at : at + 8, :] += bias_one
-        packed[at + 8 : at + 16, :] += bias_two
+        put(at, grad_one)
+        at = at + grad_one.shape[0]
+        put(at, grad_two)
+        at = at + order
+        put(at, mm(ones, one_split[0], cb=1) + mm(ones, one_split[1], cb=1))
+        put(at + 8, mm(ones, two_split[0], cb=1) + mm(ones, two_split[1], cb=1))
+        at = at + 16
+        if static and packed.shape[0] > at:
+            packed[at:, :] = jnp.zeros((packed.shape[0] - at, LANES), F32)
 
     if chunks == 1:
         chunk(0)
     else:
         mixed[...] = jnp.zeros(mixed.shape, F32)
+        packed[...] = jnp.zeros(packed.shape, F32)
 
         @pl.loop(0, chunks)
         def _(q):
@@ -350,9 +342,9 @@
     out[...] = gated.T.astype(BF16)
 
 
-def unpack_kernel(place, mine, other, grad_one, bias_one, grad_two, bias_two, grad_three, whole):
+def unpack_kernel(mine, other, grad_one, bias_one, grad_two, bias_two, grad_three, whole):
     half = mine.shape[0]
-    bit = place[1]
+    bit = lax.axis_index("dp") % 2
     whole[pl.ds(pl.multiple_of(bit * half, 8), half), :] = mine[...]
     whole[pl.ds(pl.multiple_of((1 - bit) * half, 8), half), :] = other[...]
     order = grad_three.shape[0]
@@ -370,18 +362,17 @@
     bias_two[...] = whole[at + 8 : at + 9, :]
 
 
-def run(kernel, ins, outs, scratch=(), flops=0, smem=()):
-    in_specs = [
-        pl.BlockSpec(memory_space=pltpu.SMEM if i in smem else pltpu.VMEM) for i in range(len(ins))
-    ]
+def run(kernel, ins, outs, scratch=(), flops=0, far=(), limit=SMALL):
     moved = sum(math.prod(a.shape) * a.dtype.itemsize for a in list(ins) + list(outs))
     return pl.pallas_call(
         kernel,
         out_shape=tuple(outs),
-        in_specs=in_specs,
+        in_specs=[
+            pl.BlockSpec(memory_space=pl.ANY if i in far else pltpu.VMEM) for i in range(len(ins))
+        ],
         out_specs=tuple(pl.BlockSpec(memory_space=pltpu.VMEM) for _ in outs),
         scratch_shapes=list(scratch),
-        compiler_params=pltpu.CompilerParams(vmem_limit_bytes=VMEM),
+        compiler_params=pltpu.CompilerParams(vmem_limit_bytes=limit),
         cost_estimate=pl.CostEstimate(flops=flops, bytes_accessed=moved, transcendentals=0),
     )(*ins)
 
@@ -391,7 +382,14 @@
     return lax.ppermute(block, axis, [(i, i ^ distance) for i in range(size)])
 
 
-def all_added(block):
+def all_rows(row):
+    rows = row
+    for step in range(lax.axis_size("seq").bit_length() - 1):
+        rows = jnp.concatenate([rows, swap_with(rows, "seq", 1 << step)], axis=0)
+    return rows
+
+
+def all_added(block, beside):
     steps = [("dp", 1 << i) for i in range(1, lax.axis_size("dp").bit_length() - 1)]
     steps += [("seq", 1 << i) for i in range(lax.axis_size("seq").bit_length() - 1)]
     cut = (block.shape[0] // 2 + 7) // 8 * 8
@@ -400,53 +398,70 @@
     for s in range(len(steps)):
         moves = (steps[s], steps[(s + turn) % len(steps)])
         parts = [part + swap_with(part, *move) for part, move in zip(parts, moves)]
-    return jnp.concatenate(parts, axis=0)
+        if s == 1:
+            parts[0], beside = lax.optimization_barrier((parts[0], beside))
+    return jnp.concatenate(parts, axis=0), beside
 
 
 def body(tokens, embed, taps, skip, rates, w_one, b_one, w_two, b_two, w_three, cotangent):
     blocks = lax.axis_size("seq")
-    own = lax.axis_index("seq")
-    bit = lax.axis_index("dp") % 2
     rows = tokens.shape[1]
     channels = skip.shape[0]
     features, order = w_one.shape
     length = rows * blocks
     apart = blocks > CHUNK
+    limit = LARGE if apart else SMALL
     shape = jax.ShapeDtypeStruct
-    place = jnp.stack([own, bit]).astype(jnp.int32)
-
-    gathered = lax.all_to_all(
-        jnp.broadcast_to(tokens, (blocks, rows)), "seq", split_axis=0, concat_axis=0, tiled=True
-    )
-
-    feat_high, feat_low = (jnp.asarray(t) for t in feature_tables(length, features // 2))
+
+    gathered = all_rows(tokens)
+
+    feat = jnp.asarray(feature_tables(length, features // 2))
     first, inv, sign = (jnp.asarray(t) for t in transform_tables(rows))
     code, pick = (jnp.asarray(t) for t in letter_tables(LANES))
+    rates_row = rates.reshape(1, channels)
     wide = (order, length)
-    bias_rows = (b_one.reshape(1, order), b_two.reshape(1, order))
-    pre_ins = [
-        embed[:LANES], taps, pick, rates.reshape(1, channels), skip.reshape(1, channels),
-        cotangent[0], w_one, bias_rows[0], w_two, bias_rows[1], w_three,
-    ]
-    pre_outs = [shape((3 * channels, LANES), BF16)] + [shape((channels, LANES), F32)] * 3
+    net_outs = [shape((2 * order, order), BF16), shape((2 * order, channels), BF16)]
+    if apart:
+        net_outs += [shape((2 * order, features), BF16), shape((2 * order, order), BF16)]
+        net_outs += [shape((2 * channels, order), BF16)] + [shape((order, LANES), F32)] * 2
+    else:
+        net_outs += [shape((2 * order, length), BF16), shape(wide, F32)] * 2
+        net_outs += [shape((2 * channels, order), BF16)]
+    two_back, three_back, *made = run(
+        functools.partial(network_kernel, apart),
+        [w_one, b_one.reshape(1, order), w_two, b_two.reshape(1, order), w_three, feat],
+        net_outs,
+        flops=10**9,
+        limit=limit,
+    )
+    column = shape((channels, LANES), F32)
+    table, skip_col, rates_col, cot_t = run(
+        table_kernel,
+        [embed, taps, pick, skip.reshape(1, channels), rates_row, cotangent[0]],
+        [shape((3 * channels, LANES), BF16), column, column, column],
+        scratch=[pltpu.VMEM((LANES, embed.shape[1]), embed.dtype)],
+        flops=10**9,
+        far=(0,),
+        limit=limit,
+    )
     if not apart:
-        pre_ins += [feat_high, feat_low, first]
-        pre_outs += [shape(wide, BF16), shape(wide, BF16), shape(wide, F32)] * 2
-        pre_outs += [shape((blocks, channels, 2 * rows), F32)]
-    table, rates_col, skip_col, cot_t, *made = run(
-        functools.partial(pre_kernel, length, apart), pre_ins, pre_outs, flops=2 * 10**9
-    )
+        rates_col, spectra = run(
+            functools.partial(filter_kernel, length),
+            [rates_row, made[2], made[4], first],
+            [column, shape((blocks, channels, 2 * rows), F32)],
+            flops=2 * 10**9,
+            limit=limit,
+        )
+        made[4] = spectra
 
     total = channels // LANES * order + features + order + 16
     half = (total // 2 + 7) // 8 * 8
     count = min(blocks, CHUNK)
     slots = count if blocks == count else count + 1
-    main_ins = [place, gathered, code, first, inv, sign, table, rates_col, cot_t]
-    main_ins += [w_two, w_three, feat_high, feat_low]
-    main_ins += [w_one, *bias_rows] if apart else made
     keep, send, mixed, query_t, signal_t = run(
         functools.partial(main_kernel, length, apart),
-        main_ins,
+        [gathered, table, rates_col, cot_t, feat, first, inv, sign, code, two_back, three_back]
+        + made,
         [shape((half, LANES), F32)] * 2
         + [shape((channels, 2 * rows), F32)]
         + [shape((channels, rows), F32)] * 2,
@@ -458,25 +473,25 @@
             pltpu.VMEM((2 * half, LANES), F32),
         ],
         flops=6 * 10**9,
-        smem=(0,),
-    )
-    summed = all_added(keep + swap_with(send, "dp", 1))
+        limit=limit,
+    )
     (gated,) = run(
         gate_kernel,
         [mixed, inv, query_t, signal_t, skip_col],
         [shape((rows, channels), BF16)],
         flops=3 * 10**8,
-    )
+        limit=limit,
+    )
+    summed, gated = all_added(keep + swap_with(send, "dp", 1), gated)
     other = swap_with(summed, "dp", 1)
     grad_one, bias_one, grad_two, bias_two, grad_three = run(
         unpack_kernel,
-        [place, summed, other],
+        [summed, other],
         [
             shape((features, order), F32), shape((1, order), F32), shape((order, order), F32),
             shape((1, order), F32), shape((order, channels), F32),
         ],
         scratch=[pltpu.VMEM((2 * half, LANES), F32)],
-        smem=(0,),
     )
     return (
         gated[None], grad_one, bias_one.reshape(order), grad_two, bias_two.reshape(order),

time: 61.6 us -> 54.7 us (0.89)
  Pallas kernels: 22.7 us -> 13.8 us
  waiting for transfers between devices: 9 us -> 14 us
  starting transfers between devices: 22.8 us -> 18.2 us
  local copies, waits for them, and re-layouts: 4.35 us -> 6.63 us
  other arithmetic: 1.69 us -> 0.96 us
    pallas_call x4 -> x6, Pallas kernels: 22.7 us -> 13.8 us  [run(): pl.pallas_call(kernel, out_shape=tuple(outs), in_specs=[pl.BlockSpec(memo...]
    all_to_all x1 -> x0, starting transfers between devices: 7.28 us -> none  [body(): lax.all_to_all(jnp.broadcast_to(tokens, (blocks, rows)), 'seq', split_axi...]
    unnamed x6 -> x36, local copies, waits for them, and re-layouts: 1.28 us -> 6.61 us
    ppermute x10 -> x13, waiting for transfers between devices: 9 us -> 14 us  [swap_with(): return lax.ppermute(block, axis, [(i, i ^ distance) for i in range(size)])]
    ppermute x10 -> x13, starting transfers between devices: 15.6 us -> 18.2 us  [swap_with(): return lax.ppermute(block, axis, [(i, i ^ distance) for i in range(size)])]
    slice x1 -> x0, local copies, waits for them, and re-layouts: 1.8 us -> none  [body(): embed[:LANES]]
    broadcast_in_dim x1 -> x0, local copies, waits for them, and re-layouts: 1.25 us -> none  [body(): jnp.broadcast_to(tokens, (blocks, rows))]
    add x1, other arithmetic: 0.96 us -> 0.02 us  [body(): summed, gated = all_added(keep + swap_with(send, 'dp', 1), gated)]
  transfers between devices with their start and end apart: 11 -> 13, of which waited for: 6 -> 8; matrix products, arithmetic and copies ran while one was open for 4% -> 0% of each run, Pallas kernels for 17% -> 12%
where the time goes in v2:
time: 54.7 us; the launch traced here: 54.4 us
  starting transfers between devices  18.2 us (33%)
  waiting for transfers between devices  14 us (26%)
  Pallas kernels  13.8 us (25%)
  local copies, waits for them, and re-layouts  6.63 us (12%)
  other arithmetic  0.96 us (2%)
  between operations  0.83 us (2%)
    ppermute x13, starting transfers between devices, swap_with(): return lax.ppermute(block, axis, [(i, i ^ distance) for i in range(size)])  18.2 us
    ppermute x13, waiting for transfers between devices, swap_with(): return lax.ppermute(block, axis, [(i, i ^ distance) for i in range(size)])  14 us
    pallas_call x6, Pallas kernels, run(): pl.pallas_call(kernel, out_shape=tuple(outs), in_specs=[pl.BlockSpec(memo...  13.8 us
    unnamed x36, local copies, waits for them, and re-layouts  6.61 us
  transfers between devices with their start and end apart: 13, of which 8 were waited for; matrix products, arithmetic and copies ran while one was open for 0% of the time, Pallas kernels for 12%

profile of v2, /device:TPU:0, one launch (start us, length us, event | category | flops | bytes accessed | tf_op | source)
XLA Modules:
  0.0 54.4 jit_solution(103437630842427138)
XLA Ops:
  0.6 3.0 %collective-permute-start = (s32[1,128]{1,0:T(1,128)}, s32[1,128]{1,0:T(1,128)S(1)}, u32[]{:S(2)}, u32[]{:S(2)}) collective-permute-start(s32[1,128]{1,0:T(1,128)} %param.17), channel_id=1, source_target_pairs={{0,4},{4,0},{8,12},{12,8},{16,20},{20,16},{24,28},{28,24},{1,5},{5... | collective-permute-start | bytes 1544 | tf_op jit(solution)/shard_map/ppermute | solution.py:382
  3.7 0.9 %copy-done.2 = f32[128,512]{1,0:T(8,128)S(1)} copy-done((f32[128,512]{1,0:T(8,128)S(1)}, f32[128,512]{1,0:T(8,128)}, u32[]{:S(2)}) %copy-start.2) | copy-done | bytes 262168
  4.6 0.8 %copy-done.4 = f32[128,128]{1,0:T(8,128)S(1)} copy-done((f32[128,128]{1,0:T(8,128)S(1)}, f32[128,128]{1,0:T(8,128)}, u32[]{:S(2)}) %copy-start.4) | copy-done | bytes 65560
  5.5 0.8 %copy-done.5 = f32[128,128]{1,0:T(8,128)S(1)} copy-done((f32[128,128]{1,0:T(8,128)S(1)}, f32[128,128]{1,0:T(8,128)}, u32[]{:S(2)}) %copy-start.5) | copy-done | bytes 65560
  7.6 1.0 %copy-done.11 = bf16[256,1024]{1,0:T(8,128)(2,1)S(1)} copy-done((bf16[256,1024]{1,0:T(8,128)(2,1)S(1)}, bf16[256,1024]{1,0:T(8,128)(2,1)}, u32[]{:S(2)}) %copy-start.11) | copy-done | bytes 524312
  8.7 2.1 %shard_map.209 = (bf16[256,128]{1,0:T(8,128)(2,1)S(1)}, bf16[256,512]{1,0:T(8,128)(2,1)S(1)}, bf16[256,1024]{1,0:T(8,128)(2,1)S(1)}, f32[128,1024]{1,0:T(8,128)S...) custom-call(f32[128,128]{1,0:T(8,128)S(1)} %copy-done.4, ...), custom_call_target="tpu_custom_call" | custom-call | flops 1000000000 | bytes 3605504 | tf_op jit(solution)/shard_map/pallas_call | solution.py:367
  11.6 1.6 %collective-permute-start.1 = (s32[2,128]{1,0:T(2,128)S(1)}, s32[2,128]{1,0:T(2,128)S(1)}, u32[]{:S(2)}, u32[]{:S(2)}) collective-permute-start(s32[2,128]{1,0:T(2,128)S(1)} %pad_add_fusion.2), channel_id=1, source_target_pairs={{0,8},{4,12},{8,0},{12,4},{16,24},{20,28},{24,16},{28,20},{1,9},{5... | collective-permute-start | bytes 3080 | tf_op jit(solution)/shard_map/ppermute | solution.py:382
  13.9 0.9 %copy-done.13 = bf16[256,256]{1,0:T(8,128)(2,1)S(1)} copy-done((bf16[256,256]{1,0:T(8,128)(2,1)S(1)}, bf16[256,256]{1,0:T(8,128)(2,1)}, u32[]{:S(2)}) %copy-start.13) | copy-done | bytes 131096
  14.8 2.3 %shard_map.210 = (f32[512,128]{1,0:T(8,128)S(1)}, f32[8,512,256]{2,1,0:T(8,128)S(1)}) custom-call(f32[1,512]{1,0:T(1,128)S(1)} %bitcast.10, bf16[256,1024]{1,0:T(8,128)(2,1)S(1)} %get-tuple-element.31.act_two.refs_13_, bf16[1024,128]{1,0:T(8,128)(2,1)S(1)} %get-tuple-element.32.three, bf16[256,256]{1,0:T(8,128)(2,1)S(1)} %copy-done.13), custom_call_target="tpu_custom_call" | custom-call | flops 2000000000 | bytes 5376000 | tf_op jit(solution)/shard_map/pallas_call | solution.py:367
  17.1 2.7 %collective-permute-start.2 = (s32[4,128]{1,0:T(4,128)S(1)}, s32[4,128]{1,0:T(4,128)S(1)}, u32[]{:S(2)}, u32[]{:S(2)}) collective-permute-start(s32[4,128]{1,0:T(4,128)S(1)} %pad_add_fusion.1), channel_id=1, source_target_pairs={{0,16},{4,20},{8,24},{12,28},{16,0},{20,4},{24,8},{28,12},{1,17},{... | collective-permute-start | bytes 6152 | tf_op jit(solution)/shard_map/ppermute | solution.py:382
  19.8 1.3 %shard_map.208 = (bf16[1536,128]{1,0:T(8,128)(2,1)S(1)}, f32[512,128]{1,0:T(8,128)S(1)}, f32[512,128]{1,0:T(8,128)}, f32[512,128]{1,0:T(8,128)S(1)}) custom-call(bf16[512,1536]{1,0:T(8,128)(2,1)S(1)} %copy-done.1, f32[3,3,512]{2,1,0:T(4,128)S(1)} %copy-done.6, bf16[128,128]{1,0:T(8,128)(2,1)S(1)} %copy-done.15, f32[1,512]{1,0:T(1,128)S(1)} %bitcast.9, ...), custom_call_target="tpu_custom_call" | custom-call | flops 1000000000 | bytes 2938880 | tf_op jit(solution)/shard_map/pallas_call | solution.py:367
  21.7 6.3 %shard_map.211 = (f32[392,128]{1,0:T(8,128)S(1)}, f32[392,128]{1,0:T(8,128)S(1)}, f32[512,256]{1,0:T(8,128)S(1)}, f32[512,128]{1,0:T(8,128)S(1)}, f32[512,128]{1,0:T(8,128)S(1)}) custom-call(s32[8,128]{1,0:T(8,128)S(1)} %pad_add_fusion.refs_0_, bf16[1536,128]{1,0:T(8,128)(2,1)S(1)} %get-tuple-element.30.refs_1_, f32[512,128]{1,0:T(8,128)S(1)} %get-tuple-element.33.refs_2_, ...), custom_call_target="tpu_custom_call" | custom-call | flops 6000000000 | bytes 9846784 | tf_op jit(solution)/shard_map/pallas_call | solution.py:367
  28.0 1.5 %collective-permute-done.3 = f32[392,128]{1,0:T(8,128)S(1)} collective-permute-done((f32[392,128]{1,0:T(8,128)S(1)}, f32[392,128]{1,0:T(8,128)S(1)}, u32[]{:S(2)}, u32[]{:S(2)}) %collective-permute-start.3) | collective-permute-done | bytes 200736 | tf_op jit(solution)/shard_map/ppermute | solution.py:382
  29.5 1.6 %collective-permute-start.4 = (f32[200,128]{1,0:T(8,128)S(1)}, f32[200,128]{1,0:T(8,128)S(1)}, u32[]{:S(2)}, u32[]{:S(2)}) collective-permute-start(f32[200,128]{1,0:T(8,128)S(1)} %slice.8), channel_id=1, source_target_pairs={{0,2},{1,3},{2,0},{3,1},{4,6},{5,7},{6,4},{7,5},{8,10},{9,11},{10,... | collective-permute-start | bytes 307208 | tf_op jit(solution)/shard_map/ppermute | solution.py:382
  31.6 2.9 %collective-permute-done.4 = f32[200,128]{1,0:T(8,128)S(1)} collective-permute-done((f32[200,128]{1,0:T(8,128)S(1)}, f32[200,128]{1,0:T(8,128)S(1)}, u32[]{:S(2)}, u32[]{:S(2)}) %collective-permute-start.4) | collective-permute-done | bytes 102432 | tf_op jit(solution)/shard_map/ppermute | solution.py:382
  35.8 2.7 %collective-permute-start.9 = (f32[192,128]{1,0:T(8,128)S(1)}, f32[192,128]{1,0:T(8,128)S(1)}, u32[]{:S(2)}, u32[]{:S(2)}) collective-permute-start(f32[192,128]{1,0:T(8,128)S(1)} %slice_add_fusion), channel_id=1, source_target_pairs={{0,16},{4,20},{8,24},{12,28},{16,0},{20,4},{24,8},{28,12},{1,17},{... | collective-permute-start | bytes 294920 | tf_op jit(solution)/shard_map/ppermute | solution.py:382
  38.5 1.0 %shard_map.212 = bf16[128,512]{1,0:T(8,128)(2,1)} custom-call(f32[512,256]{1,0:T(8,128)S(1)} %get-tuple-element.43.mixed, bf16[256,256]{1,0:T(8,128)(2,1)S(1)} %copy-done, f32[512,128]{1,0:T(8,128)S(1)} %get-tuple-element.44.query_t, f32[512,128]{1,0:T(8,128)S(1)} %get-tuple-element.45.signal_t, f32[512,128]{1,0:T(8,128)S(1)} %get-tuple-element.46.skip_col), custom_call_target="tpu_custom_call" | custom-call | flops 300000000 | bytes 1572864 | tf_op jit(solution)/shard_map/pallas_call | solution.py:367
  40.0 2.4 %collective-permute-done.9 = f32[192,128]{1,0:T(8,128)S(1)} collective-permute-done((f32[192,128]{1,0:T(8,128)S(1)}, f32[192,128]{1,0:T(8,128)S(1)}, u32[]{:S(2)}, u32[]{:S(2)}) %collective-permute-start.9) | collective-permute-done | bytes 98336 | tf_op jit(solution)/shard_map/ppermute | solution.py:382
  42.4 1.1 %collective-permute-start.10 = (f32[192,128]{1,0:T(8,128)S(1)}, f32[192,128]{1,0:T(8,128)S(1)}, u32[]{:S(2)}, u32[]{:S(2)}) collective-permute-start(f32[192,128]{1,0:T(8,128)S(1)} %add.33), channel_id=1, source_target_pairs={{0,2},{1,3},{2,0},{3,1},{4,6},{5,7},{6,4},{7,5},{8,10},{9,11},{10,... | collective-permute-start | bytes 294920 | tf_op jit(solution)/shard_map/ppermute | solution.py:382
  44.3 3.0 %collective-permute-start.7 = (f32[200,128]{1,0:T(8,128)S(1)}, f32[200,128]{1,0:T(8,128)S(1)}, u32[]{:S(2)}, u32[]{:S(2)}) collective-permute-start(f32[200,128]{1,0:T(8,128)S(1)} %add.30), channel_id=1, source_target_pairs={{0,16},{4,20},{8,24},{12,28},{16,0},{20,4},{24,8},{28,12},{1,17},{... | collective-permute-start | bytes 307208 | tf_op jit(solution)/shard_map/ppermute | solution.py:382
  47.3 1.0 %collective-permute-start.11 = (f32[192,128]{1,0:T(8,128)S(1)}, f32[192,128]{1,0:T(8,128)S(1)}, u32[]{:S(2)}, u32[]{:S(2)}) collective-permute-start(f32[192,128]{1,0:T(8,128)S(1)} %add.34), channel_id=1, source_target_pairs={{0,4},{4,0},{8,12},{12,8},{16,20},{20,16},{24,28},{28,24},{1,5},{5... | collective-permute-start | bytes 294920 | tf_op jit(solution)/shard_map/ppermute | solution.py:382
  48.2 3.7 %collective-permute-done.11 = f32[192,128]{1,0:T(8,128)S(1)} collective-permute-done((f32[192,128]{1,0:T(8,128)S(1)}, f32[192,128]{1,0:T(8,128)S(1)}, u32[]{:S(2)}, u32[]{:S(2)}) %collective-permute-start.11) | collective-permute-done | bytes 98336 | tf_op jit(solution)/shard_map/ppermute | solution.py:382
  52.1 1.4 %collective-permute-done.12.other = f32[392,128]{1,0:T(8,128)S(1)} collective-permute-done((f32[392,128]{1,0:T(8,128)S(1)}, f32[392,128]{1,0:T(8,128)S(1)}, u32[]{:S(2)}, u32[]{:S(2)}) %collective-permute-start.12) | collective-permute-done | bytes 200736 | tf_op jit(solution)/shard_map/ppermute | solution.py:382
  53.5 0.8 %shard_map.213 = (f32[128,128]{1,0:T(8,128)}, f32[1,128]{1,0:T(1,128)}, f32[128,128]{1,0:T(8,128)}, f32[1,128]{1,0:T(1,128)}, f32[128,512]{1,0:T(8,128)}) custom-call(f32[392,128]{1,0:T(8,128)S(1)} %pad_maximum_fusion.mine, f32[392,128]{1,0:T(8,128)S(1)} %collective-permute-done.12.other), custom_call_target="tpu_custom_call" | custom-call | bytes 795648 | tf_op jit(solution)/shard_map/pallas_call | solution.py:367
  (59 shorter events, 6.7 us)
Async XLA Ops:
  0.6 10.2 %collective-permute-start = (s32[1,128]{1,0:T(1,128)}, s32[1,128]{1,0:T(1,128)S(1)}, u32[]{:S(2)}, u32[]{:S(2)}) collective-permute-start(s32[1,128]{1,0:T(1,128)} %param.17), channel_id=1, source_target_pairs={{0,4},{4,0},{8,12},{12,8},{16,20},{20,16},{24,28},{28,24},{1,5},{5... | collective-permute-start | bytes 1544 | tf_op jit(solution)/shard_map/ppermute | solution.py:382
  7.6 1.0 %copy-start.11 = (bf16[256,1024]{1,0:T(8,128)(2,1)S(1)}, bf16[256,1024]{1,0:T(8,128)(2,1)}, u32[]{:S(2)}) copy-start(bf16[256,1024]{1,0:T(8,128)(2,1)} %constant.12.clone.feat.refs_4_) | copy-start | bytes 1572868
  8.7 8.5 %copy-start.17 = (s32[1,128]{1,0:T(1,128)S(1)}, s32[1,128]{1,0:T(1,128)}, u32[]{:S(2)}) copy-start(s32[1,128]{1,0:T(1,128)} %param.17) | copy-start | bytes 1540
  8.7 11.1 %copy-start.15 = (bf16[128,128]{1,0:T(8,128)(2,1)S(1)}, bf16[128,128]{1,0:T(8,128)(2,1)}, u32[]{:S(2)}) copy-start(bf16[128,128]{1,0:T(8,128)(2,1)} %constant.17.clone.pick) | copy-start | bytes 98308
  10.8 9.0 %copy-start.1 = (bf16[512,1536]{1,0:T(8,128)(2,1)S(1)}, bf16[512,1536]{1,0:T(8,128)(2,1)}, u32[]{:S(2)}) copy-start(bf16[512,1536]{1,0:T(8,128)(2,1)} %embed_all.1) | copy-start | bytes 4718596
  10.8 9.0 %copy-start.3 = (bf16[1,128,512]{2,1,0:T(8,128)(2,1)S(1)}, bf16[1,128,512]{2,1,0:T(8,128)(2,1)}, u32[]{:S(2)}) copy-start(bf16[1,128,512]{2,1,0:T(8,128)(2,1)} %param.27) | copy-start | bytes 393220
  10.8 9.0 %copy-start.6 = (f32[3,3,512]{2,1,0:T(4,128)S(1)}, f32[3,3,512]{2,1,0:T(4,128)}, u32[]{:S(2)}) copy-start(f32[3,3,512]{2,1,0:T(4,128)} %taps.1) | copy-start | bytes 55300
  10.8 9.0 %copy-start.7 = (f32[512]{0:T(512)S(1)}, f32[512]{0:T(512)}, u32[]{:S(2)}) copy-start(f32[512]{0:T(512)} %param.20) | copy-start | bytes 6148
  11.6 5.5 %collective-permute-start.1 = (s32[2,128]{1,0:T(2,128)S(1)}, s32[2,128]{1,0:T(2,128)S(1)}, u32[]{:S(2)}, u32[]{:S(2)}) collective-permute-start(s32[2,128]{1,0:T(2,128)S(1)} %pad_add_fusion.2), channel_id=1, source_target_pairs={{0,8},{4,12},{8,0},{12,4},{16,24},{20,28},{24,16},{28,20},{1,9},{5... | collective-permute-start | bytes 3080 | tf_op jit(solution)/shard_map/ppermute | solution.py:382
  14.8 6.9 %copy-start = (bf16[256,256]{1,0:T(8,128)(2,1)S(1)}, bf16[256,256]{1,0:T(8,128)(2,1)}, u32[]{:S(2)}) copy-start(bf16[256,256]{1,0:T(8,128)(2,1)} %constant.14.clone.refs_6_.inv) | copy-start | bytes 393220
  14.8 6.9 %copy-start.12 = (bf16[256,1024]{1,0:T(8,128)(2,1)S(1)}, bf16[256,1024]{1,0:T(8,128)(2,1)}, u32[]{:S(2)}) copy-start(bf16[256,1024]{1,0:T(8,128)(2,1)} %constant.12.clone.feat.refs_4_) | copy-start | bytes 1572868
  14.8 7.0 %copy-start.14 = (s32[128,128]{1,0:T(8,128)S(1)}, s32[128,128]{1,0:T(8,128)}, u32[]{:S(2)}) copy-start(s32[128,128]{1,0:T(8,128)} %constant.16.clone.refs_8_) | copy-start | bytes 196612
  14.8 7.0 %copy-start.16 = (f32[8,128]{1,0:T(8,128)S(1)}, f32[8,128]{1,0:T(8,128)}, u32[]{:S(2)}) copy-start(f32[8,128]{1,0:T(8,128)} %constant.15.clone.refs_7_) | copy-start | bytes 12292
  17.1 4.5 %collective-permute-start.2 = (s32[4,128]{1,0:T(4,128)S(1)}, s32[4,128]{1,0:T(4,128)S(1)}, u32[]{:S(2)}, u32[]{:S(2)}) collective-permute-start(s32[4,128]{1,0:T(4,128)S(1)} %pad_add_fusion.1), channel_id=1, source_target_pairs={{0,16},{4,20},{8,24},{12,28},{16,0},{20,4},{24,8},{28,12},{1,17},{... | collective-permute-start | bytes 6152 | tf_op jit(solution)/shard_map/ppermute | solution.py:382
  28.0 1.5 %collective-permute-start.3 = (f32[392,128]{1,0:T(8,128)S(1)}, f32[392,128]{1,0:T(8,128)S(1)}, u32[]{:S(2)}, u32[]{:S(2)}) collective-permute-start(f32[392,128]{1,0:T(8,128)S(1)} %get-tuple-element.42), channel_id=1, source_target_pairs={{0,1},{1,0},{2,3},{3,2},{4,5},{5,4},{6,7},{7,6},{8,9},{9,8},{10,11... | collective-permute-start | bytes 602120 | tf_op jit(solution)/shard_map/ppermute | solution.py:382
  29.5 5.0 %collective-permute-start.4 = (f32[200,128]{1,0:T(8,128)S(1)}, f32[200,128]{1,0:T(8,128)S(1)}, u32[]{:S(2)}, u32[]{:S(2)}) collective-permute-start(f32[200,128]{1,0:T(8,128)S(1)} %slice.8), channel_id=1, source_target_pairs={{0,2},{1,3},{2,0},{3,1},{4,6},{5,7},{6,4},{7,5},{8,10},{9,11},{10,... | collective-permute-start | bytes 307208 | tf_op jit(solution)/shard_map/ppermute | solution.py:382
  31.1 4.7 %collective-permute-start.8 = (f32[192,128]{1,0:T(8,128)S(1)}, f32[192,128]{1,0:T(8,128)S(1)}, u32[]{:S(2)}, u32[]{:S(2)}) collective-permute-start(f32[192,128]{1,0:T(8,128)S(1)} %slice.9), channel_id=1, source_target_pairs={{0,8},{4,12},{8,0},{12,4},{16,24},{20,28},{24,16},{28,20},{1,9},{5... | collective-permute-start | bytes 294920 | tf_op jit(solution)/shard_map/ppermute | solution.py:382
  34.6 5.0 %collective-permute-start.5 = (f32[200,128]{1,0:T(8,128)S(1)}, f32[200,128]{1,0:T(8,128)S(1)}, u32[]{:S(2)}, u32[]{:S(2)}) collective-permute-start(f32[200,128]{1,0:T(8,128)S(1)} %slice_add_fusion.1), channel_id=1, source_target_pairs={{0,4},{4,0},{8,12},{12,8},{16,20},{20,16},{24,28},{28,24},{1,5},{5... | collective-permute-start | bytes 307208 | tf_op jit(solution)/shard_map/ppermute | solution.py:382
  35.8 6.6 %collective-permute-start.9 = (f32[192,128]{1,0:T(8,128)S(1)}, f32[192,128]{1,0:T(8,128)S(1)}, u32[]{:S(2)}, u32[]{:S(2)}) collective-permute-start(f32[192,128]{1,0:T(8,128)S(1)} %slice_add_fusion), channel_id=1, source_target_pairs={{0,16},{4,20},{8,24},{12,28},{16,0},{20,4},{24,8},{28,12},{1,17},{... | collective-permute-start | bytes 294920 | tf_op jit(solution)/shard_map/ppermute | solution.py:382
  39.5 4.7 %collective-permute-start.6 = (f32[200,128]{1,0:T(8,128)S(1)}, f32[200,128]{1,0:T(8,128)S(1)}, u32[]{:S(2)}, u32[]{:S(2)}) collective-permute-start(f32[200,128]{1,0:T(8,128)S(1)} %add.29), channel_id=1, source_target_pairs={{0,8},{4,12},{8,0},{12,4},{16,24},{20,28},{24,16},{28,20},{1,9},{5... | collective-permute-start | bytes 307208 | tf_op jit(solution)/shard_map/ppermute | solution.py:382
  42.4 4.8 %collective-permute-start.10 = (f32[192,128]{1,0:T(8,128)S(1)}, f32[192,128]{1,0:T(8,128)S(1)}, u32[]{:S(2)}, u32[]{:S(2)}) collective-permute-start(f32[192,128]{1,0:T(8,128)S(1)} %add.33), channel_id=1, source_target_pairs={{0,2},{1,3},{2,0},{3,1},{4,6},{5,7},{6,4},{7,5},{8,10},{9,11},{10,... | collective-permute-start | bytes 294920 | tf_op jit(solution)/shard_map/ppermute | solution.py:382
  44.3 7.7 %collective-permute-start.7 = (f32[200,128]{1,0:T(8,128)S(1)}, f32[200,128]{1,0:T(8,128)S(1)}, u32[]{:S(2)}, u32[]{:S(2)}) collective-permute-start(f32[200,128]{1,0:T(8,128)S(1)} %add.30), channel_id=1, source_target_pairs={{0,16},{4,20},{8,24},{12,28},{16,0},{20,4},{24,8},{28,12},{1,17},{... | collective-permute-start | bytes 307208 | tf_op jit(solution)/shard_map/ppermute | solution.py:382
  47.3 4.7 %collective-permute-start.11 = (f32[192,128]{1,0:T(8,128)S(1)}, f32[192,128]{1,0:T(8,128)S(1)}, u32[]{:S(2)}, u32[]{:S(2)}) collective-permute-start(f32[192,128]{1,0:T(8,128)S(1)} %add.34), channel_id=1, source_target_pairs={{0,4},{4,0},{8,12},{12,8},{16,20},{20,16},{24,28},{28,24},{1,5},{5... | collective-permute-start | bytes 294920 | tf_op jit(solution)/shard_map/ppermute | solution.py:382
  52.0 1.5 %collective-permute-start.12 = (f32[392,128]{1,0:T(8,128)S(1)}, f32[392,128]{1,0:T(8,128)S(1)}, u32[]{:S(2)}, u32[]{:S(2)}) collective-permute-start(f32[392,128]{1,0:T(8,128)S(1)} %pad_maximum_fusion.mine), channel_id=1, source_target_pairs={{0,1},{1,0},{2,3},{3,2},{4,5},{5,4},{6,7},{7,6},{8,9},{9,8},{10,11... | collective-permute-start | bytes 602120 | tf_op jit(solution)/shard_map/ppermute | solution.py:382
  (7 other events, 5.5 us)

commit v3 on v2

v3 whole, which is shorter than its diff:
```python
import functools
import math

import jax
import jax.numpy as jnp
import ml_dtypes
import numpy as np
from jax import lax
from jax.experimental import pallas as pl
from jax.experimental.pallas import tpu as pltpu
from jax.sharding import PartitionSpec as P

LETTERS = (65, 67, 71, 84, 97, 99, 103, 116, 78, 110)
GROUP = 16
LANES = 128
CHUNK = 8
SMALL = 24 * 1024 * 1024
LARGE = 56 * 1024 * 1024
F32 = jnp.float32
BF16 = jnp.bfloat16


def halves(table):
    high = table.astype(np.float32).astype(ml_dtypes.bfloat16)
    low = (table - high.astype(np.float64)).astype(np.float32).astype(ml_dtypes.bfloat16)
    return high, low


def band_numbers(length, band_count):
    return [
        max(band + 1, int(0.4 * length ** (band / (band_count - 1)))) for band in range(band_count)
    ]


@functools.cache
def feature_tables(length, band_count):
    numbers = np.array(band_numbers(length, band_count), np.int64)
    residue = (numbers[:, None] * np.arange(length, dtype=np.int64)[None, :]) % length
    angles = residue * (2.0 * math.pi / length)
    return np.concatenate(halves(np.concatenate([np.sin(angles), np.cos(angles)], axis=0)), axis=0)


@functools.cache
def transform_tables(rows):
    theta = np.pi * (np.arange(rows) + 0.5) / rows
    angles = np.arange(rows)[:, None] * theta[None, :]
    forward = np.concatenate([np.cos(angles), -np.sin(angles)], axis=1)
    high, low = halves(forward)
    first = np.concatenate([high, low, high], axis=0)
    inv_high, inv_low = halves(forward.T / rows)
    inverse = np.concatenate([inv_high, inv_low], axis=1)
    sign = np.broadcast_to(np.where(np.arange(rows) % 2 == 0, 1.0, -1.0), (8, rows))
    return first, inverse, sign.astype(np.float32)


@functools.cache
def letter_tables(lanes):
    code = np.full((lanes,), -1, np.int32)
    pick = np.zeros((lanes, lanes), np.float32)
    for row in range(6 * GROUP):
        if row % GROUP < len(LETTERS):
            code[row] = LETTERS[row % GROUP]
            pick[row, code[row]] = 1.0
    code = np.ascontiguousarray(np.broadcast_to(code[:, None], (lanes, lanes)))
    return code, pick.astype(ml_dtypes.bfloat16)


def split(x):
    high = x.astype(BF16)
    return high, (x - high.astype(F32)).astype(BF16)


def mm(a, b, ca=1, cb=0):
    return lax.dot_general(a, b, (((ca,), (cb,)), ((), ())), preferred_element_type=F32)


def left_mm(stack, high, low, cb=0):
    m = stack.shape[0] // 2
    both = mm(stack, high, cb=cb)
    return both[:m] + both[m:] + mm(stack[:m], low, cb=cb)


def sin_cos(x):
    turns = jnp.floor(x * (1.0 / math.pi) + 0.5)
    r = x - turns * 3.140625
    r = r - turns * 9.67653589793116e-4
    z = r * r
    s = -0.0001980613308286788 + z * 2.599125898339353e-06
    s = -0.16666656691981288 + z * (0.00833300936890471 + z * s)
    c = 2.476157712136818e-05 + z * -2.607203341358802e-07
    c = -0.49999999533050865 + z * (0.04166664015321537 + z * (-0.0013888396896628193 + z * c))
    half = turns * 0.5
    sign = 1.0 - 4.0 * (half - jnp.floor(half))
    return sign * (r + r * z * s), sign + (sign * z) * c


def forward(block, first_ref):
    high, low = split(block)
    return mm(jnp.concatenate([high, high, low], axis=1), first_ref[...])


def inverse(real, imag, inverse_ref):
    rows = real.shape[1]
    high, low = split(jnp.concatenate([real, imag], axis=1))
    both = mm(high, inverse_ref[...])
    return both[:, :rows] + both[:, rows:] + mm(low, inverse_ref[:, :rows])


def window_block(rates, start, rows, length):
    place = (lax.broadcasted_iota(jnp.int32, (1, rows), 1) + start).astype(F32) * (-1.0 / length)
    return jnp.exp(rates * place) * (1.0 / math.sqrt(length))


def window_step(rates, rows, length):
    return jnp.exp(rates * (-rows / length))


def column_stack(weights):
    return jnp.concatenate(split(weights.T), axis=0)


def row_stack(weights):
    high, low = split(weights.T)
    return jnp.concatenate([high, high, low], axis=1)


def layer(stack, values, bias):
    size = values.shape[0] // 2
    count = values.shape[1] // LANES
    column = jnp.broadcast_to(bias, (LANES, bias.shape[1])).T
    sine, cosine = sin_cos(
        left_mm(stack, values[:size], values[size:]) + jnp.concatenate([column] * count, axis=1)
    )
    return jnp.concatenate(split(sine), axis=0), cosine


def lookup_table(embed, taps, pick):
    chosen = mm(pick, embed)
    channels = taps.shape[2]
    pieces = []
    for branch in range(3):
        part = chosen[:, branch * channels : (branch + 1) * channels]
        scaled = [
            part[tap * GROUP : (tap + 1) * GROUP] * taps[branch, tap : tap + 1, :]
            for tap in range(3)
        ]
        high = jnp.concatenate(scaled, axis=0)
        rounded = high.astype(BF16).astype(F32)
        rest = jnp.zeros((LANES - 6 * GROUP, channels), F32)
        pieces.append(jnp.concatenate([rounded, high - rounded, rest], axis=0).T)
    return jnp.concatenate(pieces, axis=0).astype(BF16)


def one_hot(tok_ref, own, block, code):
    rows = tok_ref.shape[1]

    def row(j):
        got = tok_ref[pl.ds(jnp.maximum(j, 0) ^ own, 1), :]
        return jnp.where(j >= 0, got, 0)

    now = jnp.broadcast_to(row(block), (8, rows))
    before = jnp.broadcast_to(row(block - 1), (8, rows))
    lane = lax.broadcasted_iota(jnp.int32, (8, rows), 1)
    shifted = [now]
    for tap in (1, 2):
        shifted.append(
            jnp.where(lane < tap, pltpu.roll(before, tap, 1), pltpu.roll(now, tap, 1))
        )
    wide = [jnp.concatenate([s, s], axis=0) for s in shifted]
    rest = jnp.zeros((LANES - 6 * GROUP, rows), jnp.int32)
    spread = jnp.concatenate(wide + wide + [rest], axis=0)
    return jnp.where(spread == code, 1.0, 0.0).astype(BF16)


def fetch(sources, targets, sems):
    copies = []
    for m, (source, target) in enumerate(zip(sources, targets)):
        if source.shape != target.shape:
            source = source.at[pl.ds(0, target.shape[0]), :]
        copies.append(pltpu.make_async_copy(source, target, sems.at[m]))
    for copy in copies:
        copy.start()
    return copies


def first_kernel(w_one, b_one, feat, act_one, cos_one):
    act, cosine = layer(column_stack(w_one[...]), feat[...], b_one[...])
    act_one[...] = act
    cos_one[...] = cosine


def second_kernel(apart, w_two, b_two, w_three, *refs):
    two_back, three_back = refs[-4:-2] if not apart else refs
    two_back[...] = jnp.concatenate(split(w_two[...]), axis=0)
    three_back[...] = jnp.concatenate(split(w_three[...]), axis=0)
    if not apart:
        act, cosine = layer(column_stack(w_two[...]), refs[0][...], b_two[...])
        refs[-2][...] = act
        refs[-1][...] = cosine


def table_kernel(count, *refs):
    sources, targets = refs[:count], refs[count : 2 * count - 6]
    table, skip_col, rates_col, cot_t = refs[2 * count - 6 : 2 * count - 2]
    embed, taps, pick, skip, rates, cot = refs[2 * count - 2 : -1]
    copies = fetch(sources, (embed, taps, pick, skip, rates, cot, *targets), refs[-1])
    for copy in copies[:6]:
        copy.wait()
    channels = cot.shape[1]
    table[...] = lookup_table(embed[...], taps[...], pick[...])
    skip_col[...] = jnp.broadcast_to(skip[...], (LANES, channels)).T
    rates_col[...] = jnp.broadcast_to(rates[...], (LANES, channels)).T
    cot_t[...] = cot[...].astype(F32).T
    for copy in copies[6:]:
        copy.wait()


def filter_kernel(length, rates_col, act_two, w_three, first, spectra, window, step):
    order = act_two.shape[0] // 2
    three = row_stack(w_three[...])
    window[...] = window_block(rates_col[...], 0, LANES, length)
    step[...] = window_step(rates_col[...], LANES, length)
    for k in range(0, length // LANES, 2):
        pair = min(2, length // LANES - k)
        at = slice(k * LANES, (k + pair) * LANES)
        filt = mm(three, jnp.concatenate([act_two[:, at], act_two[:order, at]], axis=0))
        for m in range(pair):
            if k + m:
                window[...] *= step[...]
            spectra[k + m] = forward(filt[:, m * LANES : (m + 1) * LANES] * window[...], first)


def shifted_sum(spec, i, slots, signs):
    rows = signs.shape[1]
    real, imag = spec[i, :, :rows], spec[i, :, rows:]
    if i + 1 < slots:
        real = real - signs * spec[i + 1, :, rows:]
        imag = imag + signs * spec[i + 1, :, :rows]
    return real, imag


def main_kernel(length, apart, *refs):
    tok = refs[0]
    table, rates_col, cot_t, feat, first, inv, sign, code, two_back, three_back = refs[1:11]
    if apart:
        w_one, b_one, w_two, b_two, w_three = refs[11:16]
        one_t, two_t = column_stack(w_one[...]), column_stack(w_two[...])
        three_t = row_stack(w_three[...])
        keep, send, query_t, signal_t, mixed, spec = refs[16:22]
    else:
        one_all, cos_one, two_all, cos_two = refs[11:15]
        keep, send, query_t, signal_t, spec = refs[15:20]
    hot, slope_high, slope_low, packed, window, step = refs[-6:]
    blocks, rows = tok.shape
    channels = cot_t.shape[0]
    order = two_back.shape[1]
    count = min(blocks, CHUNK)
    chunks = blocks // count
    own = lax.axis_index("seq")
    bit = lax.axis_index("dp") % 2
    codes = code[...]
    signs = jnp.broadcast_to(sign[0:1, :], (channels, rows))

    step[...] = window_step(rates_col[...], rows, length)
    own_hot = one_hot(tok, own, own, codes)
    query = mm(table[:channels, :], own_hot)
    query_t[...] = query
    up = forward(cot_t[...] * query, first)
    up_real, up_imag = up[:, :rows], up[:, rows:]

    def chunk(base):
        static = isinstance(base, int)
        slots = count if static else count + 1
        lane0 = base * rows if static else pl.multiple_of(base * rows, rows * count)
        for i in range(slots):
            hot[:, i * rows : (i + 1) * rows] = one_hot(tok, own, own - base - i, codes)
        span = pl.ds(lane0, count * rows)
        if apart:
            act_one, cosine_one = layer(one_t, feat[:, span], b_one[...])
            act_two, cosine_two = layer(two_t, act_one, b_two[...])
        else:
            act_one, cosine_one, act_two, cosine_two = (
                r[:, span] for r in (one_all, cos_one, two_all, cos_two)
            )
        for i in range(0, slots, 2):
            pair = min(2, slots - i)
            both = mm(table[channels:, :], hot[:, i * rows : (i + pair) * rows])
            signals = both[:channels] * both[channels:]
            for m in range(pair):
                signal = signals[:, m * rows : (m + 1) * rows]
                if i + m == 0:
                    if static:
                        signal_t[...] = signal
                    else:

                        @pl.when(base == 0)
                        def _():
                            signal_t[...] = signal

                spec[i + m] = forward(signal, first)
        for i in range(count):
            real, imag = shifted_sum(spec, i, slots, signs)
            if i == 0:
                window[...] = window_block(rates_col[...], lane0, rows, length)
            else:
                window[...] *= step[...]
            weight = window[...]
            if apart:
                at = slice(i * rows, (i + 1) * rows)
                filt = mm(three_t, jnp.concatenate([act_two[:, at], act_two[:order, at]], axis=0))
                got = forward(filt * weight, first)
                g_real, g_imag = got[:, :rows], got[:, rows:]
                mixed[:, :rows] += g_real * real - g_imag * imag
                mixed[:, rows:] += g_real * imag + g_imag * real
            lag = inverse(
                up_real * real + up_imag * imag, up_imag * real - up_real * imag, inv
            )
            high, low = split(lag * weight)
            slope_high[:, i * rows : (i + 1) * rows] = high
            slope_low[:, i * rows : (i + 1) * rows] = low

        def put(at, value):
            if static:
                packed[at : at + value.shape[0], :] = value
            else:
                packed[at : at + value.shape[0], :] += value

        slopes_high, slopes_low = slope_high[...], slope_low[...]
        grad_three = left_mm(act_two, slopes_high, slopes_low, cb=1)
        for slab in range(channels // LANES):
            put(slab * order, grad_three[:, slab * LANES : (slab + 1) * LANES])
        back_two = left_mm(three_back[...], slopes_high, slopes_low) * cosine_two
        two_split = split(back_two)
        back_one = left_mm(two_back[...], *two_split) * cosine_one
        one_split = split(back_one)
        grad_two = left_mm(act_one, *two_split, cb=1)
        grad_one = left_mm(feat[:, span], *one_split, cb=1)
        ones = jnp.ones((8, count * rows), BF16)
        at = channels // LANES * order
        put(at, grad_one)
        at = at + grad_one.shape[0]
        put(at, grad_two)
        at = at + order
        put(at, mm(ones, one_split[0], cb=1) + mm(ones, one_split[1], cb=1))
        put(at + 8, mm(ones, two_split[0], cb=1) + mm(ones, two_split[1], cb=1))
        at = at + 16
        if static and packed.shape[0] > at:
            packed[at:, :] = jnp.zeros((packed.shape[0] - at, LANES), F32)

    if chunks == 1:
        chunk(0)
    else:
        if apart:
            mixed[...] = jnp.zeros(mixed.shape, F32)
        packed[...] = jnp.zeros(packed.shape, F32)

        @pl.loop(0, chunks)
        def _(q):
            chunk(q * count)

    half = keep.shape[0]
    keep[...] = packed[pl.ds(pl.multiple_of(bit * half, 8), half), :]
    send[...] = packed[pl.ds(pl.multiple_of((1 - bit) * half, 8), half), :]


def gate_kernel(apart, *refs):
    query_t, signal_t, skip_col, inv, sign, *mix, out = refs
    rows = query_t.shape[1]
    if apart:
        total = [mix[0][:, :rows], mix[0][:, rows:]]
    else:
        spec, spectra = mix
        signs = jnp.broadcast_to(sign[0:1, :], query_t.shape)
        total = [jnp.zeros(query_t.shape, F32)] * 2
        for i in range(spec.shape[0]):
            real, imag = shifted_sum(spec, i, spec.shape[0], signs)
            g_real, g_imag = spectra[i, :, :rows], spectra[i, :, rows:]
            total[0] += g_real * real - g_imag * imag
            total[1] += g_real * imag + g_imag * real
    convolved = inverse(*total, inv)
    gated = query_t[...] * (convolved + skip_col[...] * signal_t[...])
    out[...] = gated.T.astype(BF16)


def unpack_kernel(mine, other, grad_one, bias_one, grad_two, bias_two, grad_three, whole):
    half = mine.shape[0]
    bit = lax.axis_index("dp") % 2
    whole[pl.ds(pl.multiple_of(bit * half, 8), half), :] = mine[...]
    whole[pl.ds(pl.multiple_of((1 - bit) * half, 8), half), :] = other[...]
    order = grad_three.shape[0]
    slabs = grad_three.shape[1] // LANES
    for slab in range(slabs):
        grad_three[:, slab * LANES : (slab + 1) * LANES] = whole[
            slab * order : (slab + 1) * order, :
        ]
    at = slabs * order
    features = grad_one.shape[0]
    grad_one[...] = whole[at : at + features, :]
    grad_two[...] = whole[at + features : at + features + order, :]
    at = at + features + order
    bias_one[...] = whole[at : at + 1, :]
    bias_two[...] = whole[at + 8 : at + 9, :]


def run(kernel, ins, outs, scratch=(), flops=0, far=False, limit=SMALL):
    moved = sum(math.prod(a.shape) * a.dtype.itemsize for a in list(ins) + list(outs))
    if far:
        ins = [pltpu.with_memory_space_constraint(a, pltpu.HBM) for a in ins]
    return pl.pallas_call(
        kernel,
        out_shape=tuple(outs),
        in_specs=[pl.BlockSpec(memory_space=pl.ANY if far else pltpu.VMEM)] * len(ins),
        out_specs=tuple(pl.BlockSpec(memory_space=pltpu.VMEM) for _ in outs),
        scratch_shapes=list(scratch),
        compiler_params=pltpu.CompilerParams(vmem_limit_bytes=limit),
        cost_estimate=pl.CostEstimate(flops=flops, bytes_accessed=moved, transcendentals=0),
    )(*ins)


def swap_with(block, axis, distance):
    size = lax.axis_size(axis)
    return lax.ppermute(block, axis, [(i, i ^ distance) for i in range(size)])


def all_rows(row, same_row):
    rows = jnp.concatenate([same_row, swap_with(row, "seq", 1)], axis=0)
    for step in range(1, lax.axis_size("seq").bit_length() - 1):
        rows = jnp.concatenate([rows, swap_with(rows, "seq", 1 << step)], axis=0)
    return rows


def all_added(block, first_beside, second_beside):
    steps = [("dp", 1 << i) for i in range(1, lax.axis_size("dp").bit_length() - 1)]
    steps += [("seq", 1 << i) for i in range(lax.axis_size("seq").bit_length() - 1)]
    cut = (block.shape[0] // 2 + 7) // 8 * 8
    parts = [block[:cut], block[cut:]]
    made = first_beside(block)
    turn = len(steps) // 2
    for s in range(len(steps)):
        moves = (steps[s], steps[(s + turn) % len(steps)])
        parts = [part + swap_with(part, *move) for part, move in zip(parts, moves)]
        if s == 0:
            parts[1], made = lax.optimization_barrier((parts[1], made))
            made = second_beside(made)
        if s == 1:
            parts[0], made = lax.optimization_barrier((parts[0], made))
    return jnp.concatenate(parts, axis=0), made


def body(tokens, embed, taps, skip, rates, w_one, b_one, w_two, b_two, w_three, cotangent):
    blocks = lax.axis_size("seq")
    rows = tokens.shape[1]
    channels = skip.shape[0]
    features, order = w_one.shape
    length = rows * blocks
    apart = blocks > CHUNK
    limit = LARGE if apart else SMALL
    shape = jax.ShapeDtypeStruct

    feat = jnp.asarray(feature_tables(length, features // 2))
    first, inv, sign = (jnp.asarray(t) for t in transform_tables(rows))
    code, pick = (jnp.asarray(t) for t in letter_tables(LANES))
    wide = (order, length)
    column = shape((channels, LANES), F32)
    held = [
        embed, taps, pick, skip.reshape(1, channels), rates.reshape(1, channels), cotangent[0],
        w_one, b_one.reshape(1, order), feat, w_two, b_two.reshape(1, order), w_three, tokens,
        first, inv, sign, code,
    ]
    shapes = [shape(a.shape, a.dtype) for a in held]
    shapes[0] = shape((LANES, embed.shape[1]), embed.dtype)
    near = run(
        functools.partial(table_kernel, len(held)),
        held,
        shapes[6:] + [shape((3 * channels, LANES), BF16), column, column, column],
        scratch=[pltpu.VMEM(a.shape, a.dtype) for a in shapes[:6]]
        + [pltpu.SemaphoreType.DMA((len(held),))],
        flops=5 * 10**8,
        far=True,
        limit=limit,
    )
    w_one, b_one, feat, w_two, b_two, w_three, own_tokens, first, inv, sign, code = near[:11]
    table, skip_col, rates_col, cot_t = near[11:]
    gathered = all_rows(tokens, own_tokens)
    act_one = []
    layer_outs = [] if apart else [shape((2 * order, length), BF16), shape(wide, F32)]
    if not apart:
        act_one = run(
            first_kernel, [w_one, b_one, feat], layer_outs, flops=5 * 10**8, limit=limit
        )
    two_back, three_back, *act_two = run(
        functools.partial(second_kernel, apart),
        [w_two, b_two, w_three, *act_one[:1]],
        [shape((2 * order, order), BF16), shape((2 * order, channels), BF16)] + layer_outs,
        flops=5 * 10**8,
        limit=limit,
    )

    total = channels // LANES * order + features + order + 16
    half = (total // 2 + 7) // 8 * 8
    count = min(blocks, CHUNK)
    slots = count if blocks == count else count + 1
    spec_shape = (slots, channels, 2 * rows)
    main_outs = [shape((half, LANES), F32)] * 2 + [shape((channels, rows), F32)] * 2
    scratch = [
        pltpu.VMEM((LANES, slots * rows), BF16),
        pltpu.VMEM((channels, count * rows), BF16),
        pltpu.VMEM((channels, count * rows), BF16),
        pltpu.VMEM((2 * half, LANES), F32),
        pltpu.VMEM((channels, rows), F32),
        pltpu.VMEM((channels, rows), F32),
    ]
    if apart:
        main_outs += [shape((channels, 2 * rows), F32)]
        scratch = [pltpu.VMEM(spec_shape, F32)] + scratch
    else:
        main_outs += [shape(spec_shape, F32)]
    main_ins = [gathered, table, rates_col, cot_t, feat, first, inv, sign, code, two_back]
    keep, send, query_t, signal_t, mix = run(
        functools.partial(main_kernel, length, apart),
        main_ins
        + [three_back]
        + ([w_one, b_one, w_two, b_two, w_three] if apart else [*act_one, *act_two]),
        main_outs,
        scratch=scratch,
        flops=6 * 10**9,
        limit=limit,
    )

    def first_beside(held_back):
        if apart:
            return ()
        act, _ = lax.optimization_barrier((act_two[0], held_back))
        return run(
            functools.partial(filter_kernel, length),
            [rates_col, act, w_three, first],
            [shape((blocks, channels, 2 * rows), F32)],
            scratch=[pltpu.VMEM((channels, LANES), F32)] * 2,
            flops=2 * 10**9,
            limit=limit,
        )

    def second_beside(spectra):
        (gated,) = run(
            functools.partial(gate_kernel, apart),
            [query_t, signal_t, skip_col, inv, sign, mix, *spectra],
            [shape((rows, channels), BF16)],
            flops=10**9,
            limit=limit,
        )
        return gated

    summed, gated = all_added(keep + swap_with(send, "dp", 1), first_beside, second_beside)
    other = swap_with(summed, "dp", 1)
    grad_one, bias_one, grad_two, bias_two, grad_three = run(
        unpack_kernel,
        [summed, other],
        [
            shape((features, order), F32), shape((1, order), F32), shape((order, order), F32),
            shape((1, order), F32), shape((order, channels), F32),
        ],
        scratch=[pltpu.VMEM((2 * half, LANES), F32)],
    )
    return (
        gated[None], grad_one, bias_one.reshape(order), grad_two, bias_two.reshape(order),
        grad_three,
    )


def solution(mesh):
    return jax.shard_map(
        body,
        mesh=mesh,
        in_specs=(
            P("dp", "seq"),
            P(),
            P(),
            P(),
            P(),
            P(),
            P(),
            P(),
            P(),
            P(),
            P("dp", "seq", None),
        ),
        out_specs=(P("dp", "seq", None), P(), P(), P(), P(), P()),
        check_vma=False,
    )
```

time: 54.7 us -> 48.2 us (0.88)
  local copies, waits for them, and re-layouts: 6.63 us -> 0.02 us
  starting transfers between devices: 18.2 us -> 20.3 us
  waiting for transfers between devices: 14 us -> 12 us
  Pallas kernels: 13.8 us -> 14.9 us
  other arithmetic: 0.96 us -> 0.2 us
    unnamed x36 -> x0, local copies, waits for them, and re-layouts: 6.61 us -> none
    ppermute x13, starting transfers between devices: 18.2 us -> 20.3 us  [swap_with(): return lax.ppermute(block, axis, [(i, i ^ distance) for i in range(size)])]
    ppermute x13, waiting for transfers between devices: 14 us -> 12 us  [swap_with(): return lax.ppermute(block, axis, [(i, i ^ distance) for i in range(size)])]
    pallas_call x6 -> x7, Pallas kernels: 13.8 us -> 14.9 us  [run(): pl.pallas_call(kernel, out_shape=tuple(outs), in_specs=[pl.BlockSpec(memo...]
    concatenate x3 -> x2, other arithmetic: 0.8 us -> 0.02 us  [all_rows(): rows = jnp.concatenate([rows, swap_with(rows, 'seq', 1 << step)], axis=0)]
  transfers between devices with their start and end apart: 13 -> 13, of which waited for: 8 -> 9; matrix products, arithmetic and copies ran while one was open for 0% -> 0% of each run, Pallas kernels for 12% -> 16%
where the time goes in v3:
time: 48.2 us; the launch traced here: 48.1 us
  starting transfers between devices  20.3 us (42%)
  Pallas kernels  14.9 us (31%)
  waiting for transfers between devices  12 us (25%)
  between operations  0.74 us (2%)
    ppermute x13, starting transfers between devices, swap_with(): return lax.ppermute(block, axis, [(i, i ^ distance) for i in range(size)])  20.3 us
    pallas_call x7, Pallas kernels, run(): pl.pallas_call(kernel, out_shape=tuple(outs), in_specs=[pl.BlockSpec(memo...  14.9 us
    ppermute x13, waiting for transfers between devices, swap_with(): return lax.ppermute(block, axis, [(i, i ^ distance) for i in range(size)])  12 us
  transfers between devices with their start and end apart: 13, of which 9 were waited for; matrix products, arithmetic and copies ran while one was open for 0% of the time, Pallas kernels for 16%

profile of v3, /device:TPU:0, one launch (start us, length us, event | category | flops | bytes accessed | tf_op | source)
XLA Modules:
  0.0 48.1 jit_solution(297946095769390508)
XLA Ops:
  0.6 3.0 %collective-permute-start = (s32[1,128]{1,0:T(1,128)}, s32[1,128]{1,0:T(1,128)S(1)}, u32[]{:S(2)}, u32[]{:S(2)}) collective-permute-start(s32[1,128]{1,0:T(1,128)} %refs_12_.1), channel_id=1, source_target_pairs={{0,4},{4,0},{8,12},{12,8},{16,20},{20,16},{24,28},{28,24},{1,5},{5... | collective-permute-start | bytes 1544 | tf_op jit(solution)/shard_map/ppermute | solution.py:422
  3.7 1.7 %shard_map.208 = (f32[128,128]{1,0:T(8,128)S(1)}, f32[1,128]{1,0:T(1,128)S(1)}, bf16[256,1024]{1,0:T(8,128)(2,1)S(1)}, f32[128,128]{1,0:T(8,128)S(1)}, f32[1,128...) custom-call(bf16[512,1536]{1,0:T(8,128)(2,1)} %refs_0_.1, ...), custom_call_target="tpu_custom_call" | custom-call | flops 500000000 | bytes 5571584 | tf_op jit(solution)/shard_map/pallas_call | solution.py:409
  5.4 2.0 %collective-permute-start.1 = (s32[2,128]{1,0:T(2,128)S(1)}, s32[2,128]{1,0:T(2,128)S(1)}, u32[]{:S(2)}, u32[]{:S(2)}) collective-permute-start(s32[2,128]{1,0:T(2,128)S(1)} %pad_add_fusion.2), channel_id=1, source_target_pairs={{0,8},{4,12},{8,0},{12,4},{16,24},{20,28},{24,16},{28,20},{1,9},{5... | collective-permute-start | bytes 3080 | tf_op jit(solution)/shard_map/ppermute | solution.py:422
  7.4 1.0 %shard_map.209 = (bf16[256,1024]{1,0:T(8,128)(2,1)S(1)}, f32[128,1024]{1,0:T(8,128)S(1)}) custom-call(f32[128,128]{1,0:T(8,128)S(1)} %get-tuple-element.54.w_one, f32[1,128]{1,0:T(1,128)S(1)} %get-tuple-element.55.b_one, bf16[256,1024]{1,0:T(8,128)(2,1)S(1)} %get-tuple-element.46.feat.refs_4_), custom_call_target="tpu_custom_call" | custom-call | flops 500000000 | bytes 1638912 | tf_op jit(solution)/shard_map/pallas_call | solution.py:409
  8.4 0.6 %collective-permute-done.1 = s32[2,128]{1,0:T(2,128)S(1)} collective-permute-done((s32[2,128]{1,0:T(2,128)S(1)}, s32[2,128]{1,0:T(2,128)S(1)}, u32[]{:S(2)}, u32[]{:S(2)}) %collective-permute-start.1) | collective-permute-done | bytes 1056 | tf_op jit(solution)/shard_map/ppermute | solution.py:422
  9.0 3.1 %collective-permute-start.2 = (s32[4,128]{1,0:T(4,128)S(1)}, s32[4,128]{1,0:T(4,128)S(1)}, u32[]{:S(2)}, u32[]{:S(2)}) collective-permute-start(s32[4,128]{1,0:T(4,128)S(1)} %pad_add_fusion.1), channel_id=1, source_target_pairs={{0,16},{4,20},{8,24},{12,28},{16,0},{20,4},{24,8},{28,12},{1,17},{... | collective-permute-start | bytes 6152 | tf_op jit(solution)/shard_map/ppermute | solution.py:422
  12.1 1.0 %shard_map.210 = (bf16[256,128]{1,0:T(8,128)(2,1)S(1)}, bf16[256,512]{1,0:T(8,128)(2,1)S(1)}, bf16[256,1024]{1,0:T(8,128)(2,1)S(1)}, f32[128,1024]{1,0:T(8,128)S(1)}) custom-call(f32[128,128]{1,0:T(8,128)S(1)} %get-tuple-element.51.w_two, f32[1,128]{1,0:T(1,128)S(1)} %get-tuple-element.52.b_two, f32[128,512]{1,0:T(8,128)S(1)} %get-tuple-element.53.w_three, ...), custom_call_target="tpu_custom_call" | custom-call | flops 500000000 | bytes 2228736 | tf_op jit(solution)/shard_map/pallas_call | solution.py:409
  13.6 6.2 %shard_map.211 = (f32[392,128]{1,0:T(8,128)S(1)}, f32[392,128]{1,0:T(8,128)S(1)}, f32[512,128]{1,0:T(8,128)S(1)}, f32[512,128]{1,0:T(8,128)S(1)}, f32[8,512,256]{2,1,0:T(8,128)S(1)}) custom-call(s32[8,128]{1,0:T(8,128)S(1)} %pad_add_fusion.refs_0_, bf16[1536,128]{1,0:T(8,128)(2,1)S(1)} %get-tuple-element.43.refs_1_, ...), custom_call_target="tpu_custom_call" | custom-call | flops 6000000000 | bytes 9388032 | tf_op jit(solution)/shard_map/pallas_call | solution.py:409
  19.9 1.5 %collective-permute-done.3 = f32[392,128]{1,0:T(8,128)S(1)} collective-permute-done((f32[392,128]{1,0:T(8,128)S(1)}, f32[392,128]{1,0:T(8,128)S(1)}, u32[]{:S(2)}, u32[]{:S(2)}) %collective-permute-start.3) | collective-permute-done | bytes 200736 | tf_op jit(solution)/shard_map/ppermute | solution.py:422
  21.4 2.0 %collective-permute-start.6 = (f32[192,128]{1,0:T(8,128)S(1)}, f32[192,128]{1,0:T(8,128)S(1)}, u32[]{:S(2)}, u32[]{:S(2)}) collective-permute-start(f32[192,128]{1,0:T(8,128)S(1)} %slice.9), channel_id=1, source_target_pairs={{0,8},{4,12},{8,0},{12,4},{16,24},{20,28},{24,16},{28,20},{1,9},{5... | collective-permute-start | bytes 294920 | tf_op jit(solution)/shard_map/ppermute | solution.py:422
  23.4 1.5 %collective-permute-start.4 = (f32[200,128]{1,0:T(8,128)S(1)}, f32[200,128]{1,0:T(8,128)S(1)}, u32[]{:S(2)}, u32[]{:S(2)}) collective-permute-start(f32[200,128]{1,0:T(8,128)S(1)} %slice.8), channel_id=1, source_target_pairs={{0,2},{1,3},{2,0},{3,1},{4,6},{5,7},{6,4},{7,5},{8,10},{9,11},{10,... | collective-permute-start | bytes 307208 | tf_op jit(solution)/shard_map/ppermute | solution.py:422
  24.9 2.3 %shard_map.212.refs_6_ = f32[8,512,256]{2,1,0:T(8,128)S(1)} custom-call(f32[512,128]{1,0:T(8,128)S(1)} %get-tuple-element.44.refs_2_.rates_col, bf16[256,1024]{1,0:T(8,128)(2,1)S(1)} %get-tuple-element.68.refs_13_.act_two, f32[128,512]{1,0:T(8,128)S(1)} %get-tuple-element.53.w_three, bf16[384,256]{1,0:T(8,128)(2,1)S(1)} %get-tuple-element.47.refs_5_.first), custom_call_target="tpu_custom_call" | custom-call | flops 2000000000 | bytes 5439488 | tf_op jit(solution)/shard_map/pallas_call | solution.py:409
  27.2 0.8 %collective-permute-done.4 = f32[200,128]{1,0:T(8,128)S(1)} collective-permute-done((f32[200,128]{1,0:T(8,128)S(1)}, f32[200,128]{1,0:T(8,128)S(1)}, u32[]{:S(2)}, u32[]{:S(2)}) %collective-permute-start.4) | collective-permute-done | bytes 102432 | tf_op jit(solution)/shard_map/ppermute | solution.py:422
  28.0 1.6 %collective-permute-start.5 = (f32[200,128]{1,0:T(8,128)S(1)}, f32[200,128]{1,0:T(8,128)S(1)}, u32[]{:S(2)}, u32[]{:S(2)}) collective-permute-start(f32[200,128]{1,0:T(8,128)S(1)} %slice_add_fusion.1), channel_id=1, source_target_pairs={{0,4},{4,0},{8,12},{12,8},{16,20},{20,16},{24,28},{28,24},{1,5},{5... | collective-permute-start | bytes 307208 | tf_op jit(solution)/shard_map/ppermute | solution.py:422
  29.6 2.7 %collective-permute-start.9 = (f32[192,128]{1,0:T(8,128)S(1)}, f32[192,128]{1,0:T(8,128)S(1)}, u32[]{:S(2)}, u32[]{:S(2)}) collective-permute-start(f32[192,128]{1,0:T(8,128)S(1)} %slice_add_fusion), channel_id=1, source_target_pairs={{0,16},{4,20},{8,24},{12,28},{16,0},{20,4},{24,8},{28,12},{1,17},{... | collective-permute-start | bytes 294920 | tf_op jit(solution)/shard_map/ppermute | solution.py:422
  32.3 1.8 %shard_map.213 = bf16[128,512]{1,0:T(8,128)(2,1)} custom-call(f32[512,128]{1,0:T(8,128)S(1)} %get-tuple-element.64.refs_0_, f32[512,128]{1,0:T(8,128)S(1)} %get-tuple-element.65.refs_1_, f32[512,128]{1,0:T(8,128)S(1)} %get-tuple-element.66.refs_2_, bf16[256,256]{1,0:T(8,128)(2,1)S(1)} %get-tuple-element.48.refs_6_.refs_3_, ...), custom_call_target="tpu_custom_call" | custom-call | flops 1000000000 | bytes 9441280 | tf_op jit(solution)/shard_map/pallas_call | solution.py:409
  34.7 1.6 %collective-permute-done.9 = f32[192,128]{1,0:T(8,128)S(1)} collective-permute-done((f32[192,128]{1,0:T(8,128)S(1)}, f32[192,128]{1,0:T(8,128)S(1)}, u32[]{:S(2)}, u32[]{:S(2)}) %collective-permute-start.9) | collective-permute-done | bytes 98336 | tf_op jit(solution)/shard_map/ppermute | solution.py:422
  36.3 1.6 %collective-permute-start.10 = (f32[192,128]{1,0:T(8,128)S(1)}, f32[192,128]{1,0:T(8,128)S(1)}, u32[]{:S(2)}, u32[]{:S(2)}) collective-permute-start(f32[192,128]{1,0:T(8,128)S(1)} %add.33), channel_id=1, source_target_pairs={{0,2},{1,3},{2,0},{3,1},{4,6},{5,7},{6,4},{7,5},{8,10},{9,11},{10,... | collective-permute-start | bytes 294920 | tf_op jit(solution)/shard_map/ppermute | solution.py:422
  37.8 1.0 %collective-permute-done.7 = f32[200,128]{1,0:T(8,128)S(1)} collective-permute-done((f32[200,128]{1,0:T(8,128)S(1)}, f32[200,128]{1,0:T(8,128)S(1)}, u32[]{:S(2)}, u32[]{:S(2)}) %collective-permute-start.7) | collective-permute-done | bytes 102432 | tf_op jit(solution)/shard_map/ppermute | solution.py:422
  38.9 1.5 %collective-permute-start.8 = (f32[200,128]{1,0:T(8,128)S(1)}, f32[200,128]{1,0:T(8,128)S(1)}, u32[]{:S(2)}, u32[]{:S(2)}) collective-permute-start(f32[200,128]{1,0:T(8,128)S(1)} %add.31), channel_id=1, source_target_pairs={{0,16},{4,20},{8,24},{12,28},{16,0},{20,4},{24,8},{28,12},{1,17},{... | collective-permute-start | bytes 307208 | tf_op jit(solution)/shard_map/ppermute | solution.py:422
  41.0 0.8 %collective-permute-start.11 = (f32[192,128]{1,0:T(8,128)S(1)}, f32[192,128]{1,0:T(8,128)S(1)}, u32[]{:S(2)}, u32[]{:S(2)}) collective-permute-start(f32[192,128]{1,0:T(8,128)S(1)} %add.34), channel_id=1, source_target_pairs={{0,4},{4,0},{8,12},{12,8},{16,20},{20,16},{24,28},{28,24},{1,5},{5... | collective-permute-start | bytes 294920 | tf_op jit(solution)/shard_map/ppermute | solution.py:422
  41.8 3.9 %collective-permute-done.11 = f32[192,128]{1,0:T(8,128)S(1)} collective-permute-done((f32[192,128]{1,0:T(8,128)S(1)}, f32[192,128]{1,0:T(8,128)S(1)}, u32[]{:S(2)}, u32[]{:S(2)}) %collective-permute-start.11) | collective-permute-done | bytes 98336 | tf_op jit(solution)/shard_map/ppermute | solution.py:422
  45.8 1.4 %collective-permute-done.12.other = f32[392,128]{1,0:T(8,128)S(1)} collective-permute-done((f32[392,128]{1,0:T(8,128)S(1)}, f32[392,128]{1,0:T(8,128)S(1)}, u32[]{:S(2)}, u32[]{:S(2)}) %collective-permute-start.12) | collective-permute-done | bytes 200736 | tf_op jit(solution)/shard_map/ppermute | solution.py:422
  47.3 0.8 %shard_map.214 = (f32[128,128]{1,0:T(8,128)}, f32[1,128]{1,0:T(1,128)}, f32[128,128]{1,0:T(8,128)}, f32[1,128]{1,0:T(1,128)}, f32[128,512]{1,0:T(8,128)}) custom-call(f32[392,128]{1,0:T(8,128)S(1)} %pad_maximum_fusion.mine, f32[392,128]{1,0:T(8,128)S(1)} %collective-permute-done.12.other), custom_call_target="tpu_custom_call" | custom-call | bytes 795648 | tf_op jit(solution)/shard_map/pallas_call | solution.py:409
  (24 shorter events, 1.9 us)
Async XLA Ops:
  0.6 4.7 %collective-permute-start = (s32[1,128]{1,0:T(1,128)}, s32[1,128]{1,0:T(1,128)S(1)}, u32[]{:S(2)}, u32[]{:S(2)}) collective-permute-start(s32[1,128]{1,0:T(1,128)} %refs_12_.1), channel_id=1, source_target_pairs={{0,4},{4,0},{8,12},{12,8},{16,20},{20,16},{24,28},{28,24},{1,5},{5... | collective-permute-start | bytes 1544 | tf_op jit(solution)/shard_map/ppermute | solution.py:422
  5.4 3.6 %collective-permute-start.1 = (s32[2,128]{1,0:T(2,128)S(1)}, s32[2,128]{1,0:T(2,128)S(1)}, u32[]{:S(2)}, u32[]{:S(2)}) collective-permute-start(s32[2,128]{1,0:T(2,128)S(1)} %pad_add_fusion.2), channel_id=1, source_target_pairs={{0,8},{4,12},{8,0},{12,4},{16,24},{20,28},{24,16},{28,20},{1,9},{5... | collective-permute-start | bytes 3080 | tf_op jit(solution)/shard_map/ppermute | solution.py:422
  9.0 4.6 %collective-permute-start.2 = (s32[4,128]{1,0:T(4,128)S(1)}, s32[4,128]{1,0:T(4,128)S(1)}, u32[]{:S(2)}, u32[]{:S(2)}) collective-permute-start(s32[4,128]{1,0:T(4,128)S(1)} %pad_add_fusion.1), channel_id=1, source_target_pairs={{0,16},{4,20},{8,24},{12,28},{16,0},{20,4},{24,8},{28,12},{1,17},{... | collective-permute-start | bytes 6152 | tf_op jit(solution)/shard_map/ppermute | solution.py:422
  19.8 1.5 %collective-permute-start.3 = (f32[392,128]{1,0:T(8,128)S(1)}, f32[392,128]{1,0:T(8,128)S(1)}, u32[]{:S(2)}, u32[]{:S(2)}) collective-permute-start(f32[392,128]{1,0:T(8,128)S(1)} %get-tuple-element.63), channel_id=1, source_target_pairs={{0,1},{1,0},{2,3},{3,2},{4,5},{5,4},{6,7},{7,6},{8,9},{9,8},{10,11... | collective-permute-start | bytes 602120 | tf_op jit(solution)/shard_map/ppermute | solution.py:422
  21.4 8.2 %collective-permute-start.6 = (f32[192,128]{1,0:T(8,128)S(1)}, f32[192,128]{1,0:T(8,128)S(1)}, u32[]{:S(2)}, u32[]{:S(2)}) collective-permute-start(f32[192,128]{1,0:T(8,128)S(1)} %slice.9), channel_id=1, source_target_pairs={{0,8},{4,12},{8,0},{12,4},{16,24},{20,28},{24,16},{28,20},{1,9},{5... | collective-permute-start | bytes 294920 | tf_op jit(solution)/shard_map/ppermute | solution.py:422
  23.4 4.7 %collective-permute-start.4 = (f32[200,128]{1,0:T(8,128)S(1)}, f32[200,128]{1,0:T(8,128)S(1)}, u32[]{:S(2)}, u32[]{:S(2)}) collective-permute-start(f32[200,128]{1,0:T(8,128)S(1)} %slice.8), channel_id=1, source_target_pairs={{0,2},{1,3},{2,0},{3,1},{4,6},{5,7},{6,4},{7,5},{8,10},{9,11},{10,... | collective-permute-start | bytes 307208 | tf_op jit(solution)/shard_map/ppermute | solution.py:422
  28.0 6.1 %collective-permute-start.5 = (f32[200,128]{1,0:T(8,128)S(1)}, f32[200,128]{1,0:T(8,128)S(1)}, u32[]{:S(2)}, u32[]{:S(2)}) collective-permute-start(f32[200,128]{1,0:T(8,128)S(1)} %slice_add_fusion.1), channel_id=1, source_target_pairs={{0,4},{4,0},{8,12},{12,8},{16,20},{20,16},{24,28},{28,24},{1,5},{5... | collective-permute-start | bytes 307208 | tf_op jit(solution)/shard_map/ppermute | solution.py:422
  29.6 6.6 %collective-permute-start.9 = (f32[192,128]{1,0:T(8,128)S(1)}, f32[192,128]{1,0:T(8,128)S(1)}, u32[]{:S(2)}, u32[]{:S(2)}) collective-permute-start(f32[192,128]{1,0:T(8,128)S(1)} %slice_add_fusion), channel_id=1, source_target_pairs={{0,16},{4,20},{8,24},{12,28},{16,0},{20,4},{24,8},{28,12},{1,17},{... | collective-permute-start | bytes 294920 | tf_op jit(solution)/shard_map/ppermute | solution.py:422
  34.2 4.7 %collective-permute-start.7 = (f32[200,128]{1,0:T(8,128)S(1)}, f32[200,128]{1,0:T(8,128)S(1)}, u32[]{:S(2)}, u32[]{:S(2)}) collective-permute-start(f32[200,128]{1,0:T(8,128)S(1)} %add.29), channel_id=1, source_target_pairs={{0,8},{4,12},{8,0},{12,4},{16,24},{20,28},{24,16},{28,20},{1,9},{5... | collective-permute-start | bytes 307208 | tf_op jit(solution)/shard_map/ppermute | solution.py:422
  36.3 4.7 %collective-permute-start.10 = (f32[192,128]{1,0:T(8,128)S(1)}, f32[192,128]{1,0:T(8,128)S(1)}, u32[]{:S(2)}, u32[]{:S(2)}) collective-permute-start(f32[192,128]{1,0:T(8,128)S(1)} %add.33), channel_id=1, source_target_pairs={{0,2},{1,3},{2,0},{3,1},{4,6},{5,7},{6,4},{7,5},{8,10},{9,11},{10,... | collective-permute-start | bytes 294920 | tf_op jit(solution)/shard_map/ppermute | solution.py:422
  38.9 6.8 %collective-permute-start.8 = (f32[200,128]{1,0:T(8,128)S(1)}, f32[200,128]{1,0:T(8,128)S(1)}, u32[]{:S(2)}, u32[]{:S(2)}) collective-permute-start(f32[200,128]{1,0:T(8,128)S(1)} %add.31), channel_id=1, source_target_pairs={{0,16},{4,20},{8,24},{12,28},{16,0},{20,4},{24,8},{28,12},{1,17},{... | collective-permute-start | bytes 307208 | tf_op jit(solution)/shard_map/ppermute | solution.py:422
  41.0 4.7 %collective-permute-start.11 = (f32[192,128]{1,0:T(8,128)S(1)}, f32[192,128]{1,0:T(8,128)S(1)}, u32[]{:S(2)}, u32[]{:S(2)}) collective-permute-start(f32[192,128]{1,0:T(8,128)S(1)} %add.34), channel_id=1, source_target_pairs={{0,4},{4,0},{8,12},{12,8},{16,20},{20,16},{24,28},{28,24},{1,5},{5... | collective-permute-start | bytes 294920 | tf_op jit(solution)/shard_map/ppermute | solution.py:422
  45.7 1.5 %collective-permute-start.12 = (f32[392,128]{1,0:T(8,128)S(1)}, f32[392,128]{1,0:T(8,128)S(1)}, u32[]{:S(2)}, u32[]{:S(2)}) collective-permute-start(f32[392,128]{1,0:T(8,128)S(1)} %pad_maximum_fusion.mine), channel_id=1, source_target_pairs={{0,1},{1,0},{2,3},{3,2},{4,5},{5,4},{6,7},{7,6},{8,9},{9,8},{10,11... | collective-permute-start | bytes 602120 | tf_op jit(solution)/shard_map/ppermute | solution.py:422

commit v4 on v3

--- a/solution.py
+++ b/solution.py
@@ -286,18 +286,19 @@
             pair = min(2, slots - i)
             both = mm(table[channels:, :], hot[:, i * rows : (i + pair) * rows])
             signals = both[:channels] * both[channels:]
+            parts = [signals[:, m * rows : (m + 1) * rows] for m in range(pair)]
+            if i == 0:
+                if static:
+                    signal_t[...] = parts[0]
+                else:
+
+                    @pl.when(base == 0)
+                    def _():
+                        signal_t[...] = parts[0]
+
+            made = forward(jnp.concatenate(parts, axis=0), first)
             for m in range(pair):
-                signal = signals[:, m * rows : (m + 1) * rows]
-                if i + m == 0:
-                    if static:
-                        signal_t[...] = signal
-                    else:
-
-                        @pl.when(base == 0)
-                        def _():
-                            signal_t[...] = signal
-
-                spec[i + m] = forward(signal, first)
+                spec[i + m] = made[m * channels : (m + 1) * channels]
         for i in range(count):
             real, imag = shifted_sum(spec, i, slots, signs)
             if i == 0:

time: 48.2 us -> 47.7 us (0.990)
  Pallas kernels: 14.9 us -> 14.3 us
    pallas_call x7, Pallas kernels: 14.9 us -> 14.3 us  [run(): pl.pallas_call(kernel, out_shape=tuple(outs), in_specs=[pl.BlockSpec(memo...]
where the time goes in v4:
time: 47.7 us; the launch traced here: 47.5 us
  starting transfers between devices  20.3 us (43%)
  Pallas kernels  14.3 us (30%)
  waiting for transfers between devices  12 us (25%)
  between operations  0.74 us (2%)
    ppermute x13, starting transfers between devices, swap_with(): return lax.ppermute(block, axis, [(i, i ^ distance) for i in range(size)])  20.3 us
    pallas_call x7, Pallas kernels, run(): pl.pallas_call(kernel, out_shape=tuple(outs), in_specs=[pl.BlockSpec(memo...  14.3 us
    ppermute x13, waiting for transfers between devices, swap_with(): return lax.ppermute(block, axis, [(i, i ^ distance) for i in range(size)])  12 us
  transfers between devices with their start and end apart: 13, of which 9 were waited for; matrix products, arithmetic and copies ran while one was open for 0% of the time, Pallas kernels for 16%

profile of v4, /device:TPU:0, one launch (start us, length us, event | category | flops | bytes accessed | tf_op | source)
XLA Modules:
  0.0 47.5 jit_solution(3723282055537986677)
XLA Ops:
  0.6 3.0 %collective-permute-start = (s32[1,128]{1,0:T(1,128)}, s32[1,128]{1,0:T(1,128)S(1)}, u32[]{:S(2)}, u32[]{:S(2)}) collective-permute-start(s32[1,128]{1,0:T(1,128)} %refs_12_.1), channel_id=1, source_target_pairs={{0,4},{4,0},{8,12},{12,8},{16,20},{20,16},{24,28},{28,24},{1,5},{5... | collective-permute-start | bytes 1544 | tf_op jit(solution)/shard_map/ppermute | solution.py:423
  3.7 1.7 %shard_map.208 = (f32[128,128]{1,0:T(8,128)S(1)}, f32[1,128]{1,0:T(1,128)S(1)}, bf16[256,1024]{1,0:T(8,128)(2,1)S(1)}, f32[128,128]{1,0:T(8,128)S(1)}, f32[1,128...) custom-call(bf16[512,1536]{1,0:T(8,128)(2,1)} %refs_0_.1, ...), custom_call_target="tpu_custom_call" | custom-call | flops 500000000 | bytes 5571584 | tf_op jit(solution)/shard_map/pallas_call | solution.py:410
  5.4 2.0 %collective-permute-start.1 = (s32[2,128]{1,0:T(2,128)S(1)}, s32[2,128]{1,0:T(2,128)S(1)}, u32[]{:S(2)}, u32[]{:S(2)}) collective-permute-start(s32[2,128]{1,0:T(2,128)S(1)} %pad_add_fusion.2), channel_id=1, source_target_pairs={{0,8},{4,12},{8,0},{12,4},{16,24},{20,28},{24,16},{28,20},{1,9},{5... | collective-permute-start | bytes 3080 | tf_op jit(solution)/shard_map/ppermute | solution.py:423
  7.4 1.0 %shard_map.209 = (bf16[256,1024]{1,0:T(8,128)(2,1)S(1)}, f32[128,1024]{1,0:T(8,128)S(1)}) custom-call(f32[128,128]{1,0:T(8,128)S(1)} %get-tuple-element.54.w_one, f32[1,128]{1,0:T(1,128)S(1)} %get-tuple-element.55.b_one, bf16[256,1024]{1,0:T(8,128)(2,1)S(1)} %get-tuple-element.46.feat.refs_4_), custom_call_target="tpu_custom_call" | custom-call | flops 500000000 | bytes 1638912 | tf_op jit(solution)/shard_map/pallas_call | solution.py:410
  8.4 0.6 %collective-permute-done.1 = s32[2,128]{1,0:T(2,128)S(1)} collective-permute-done((s32[2,128]{1,0:T(2,128)S(1)}, s32[2,128]{1,0:T(2,128)S(1)}, u32[]{:S(2)}, u32[]{:S(2)}) %collective-permute-start.1) | collective-permute-done | bytes 1056 | tf_op jit(solution)/shard_map/ppermute | solution.py:423
  9.0 3.1 %collective-permute-start.2 = (s32[4,128]{1,0:T(4,128)S(1)}, s32[4,128]{1,0:T(4,128)S(1)}, u32[]{:S(2)}, u32[]{:S(2)}) collective-permute-start(s32[4,128]{1,0:T(4,128)S(1)} %pad_add_fusion.1), channel_id=1, source_target_pairs={{0,16},{4,20},{8,24},{12,28},{16,0},{20,4},{24,8},{28,12},{1,17},{... | collective-permute-start | bytes 6152 | tf_op jit(solution)/shard_map/ppermute | solution.py:423
  12.1 1.0 %shard_map.210 = (bf16[256,128]{1,0:T(8,128)(2,1)S(1)}, bf16[256,512]{1,0:T(8,128)(2,1)S(1)}, bf16[256,1024]{1,0:T(8,128)(2,1)S(1)}, f32[128,1024]{1,0:T(8,128)S(1)}) custom-call(f32[128,128]{1,0:T(8,128)S(1)} %get-tuple-element.51.w_two, f32[1,128]{1,0:T(1,128)S(1)} %get-tuple-element.52.b_two, f32[128,512]{1,0:T(8,128)S(1)} %get-tuple-element.53.w_three, ...), custom_call_target="tpu_custom_call" | custom-call | flops 500000000 | bytes 2228736 | tf_op jit(solution)/shard_map/pallas_call | solution.py:410
  13.6 5.7 %shard_map.211 = (f32[392,128]{1,0:T(8,128)S(1)}, f32[392,128]{1,0:T(8,128)S(1)}, f32[512,128]{1,0:T(8,128)S(1)}, f32[512,128]{1,0:T(8,128)S(1)}, f32[8,512,256]{2,1,0:T(8,128)S(1)}) custom-call(s32[8,128]{1,0:T(8,128)S(1)} %pad_add_fusion.refs_0_, bf16[1536,128]{1,0:T(8,128)(2,1)S(1)} %get-tuple-element.43.refs_1_, ...), custom_call_target="tpu_custom_call" | custom-call | flops 6000000000 | bytes 9388032 | tf_op jit(solution)/shard_map/pallas_call | solution.py:410
  19.3 1.5 %collective-permute-done.3 = f32[392,128]{1,0:T(8,128)S(1)} collective-permute-done((f32[392,128]{1,0:T(8,128)S(1)}, f32[392,128]{1,0:T(8,128)S(1)}, u32[]{:S(2)}, u32[]{:S(2)}) %collective-permute-start.3) | collective-permute-done | bytes 200736 | tf_op jit(solution)/shard_map/ppermute | solution.py:423
  20.9 2.0 %collective-permute-start.6 = (f32[192,128]{1,0:T(8,128)S(1)}, f32[192,128]{1,0:T(8,128)S(1)}, u32[]{:S(2)}, u32[]{:S(2)}) collective-permute-start(f32[192,128]{1,0:T(8,128)S(1)} %slice.9), channel_id=1, source_target_pairs={{0,8},{4,12},{8,0},{12,4},{16,24},{20,28},{24,16},{28,20},{1,9},{5... | collective-permute-start | bytes 294920 | tf_op jit(solution)/shard_map/ppermute | solution.py:423
  22.8 1.5 %collective-permute-start.4 = (f32[200,128]{1,0:T(8,128)S(1)}, f32[200,128]{1,0:T(8,128)S(1)}, u32[]{:S(2)}, u32[]{:S(2)}) collective-permute-start(f32[200,128]{1,0:T(8,128)S(1)} %slice.8), channel_id=1, source_target_pairs={{0,2},{1,3},{2,0},{3,1},{4,6},{5,7},{6,4},{7,5},{8,10},{9,11},{10,... | collective-permute-start | bytes 307208 | tf_op jit(solution)/shard_map/ppermute | solution.py:423
  24.3 2.3 %shard_map.212.refs_6_ = f32[8,512,256]{2,1,0:T(8,128)S(1)} custom-call(f32[512,128]{1,0:T(8,128)S(1)} %get-tuple-element.44.refs_2_.rates_col, bf16[256,1024]{1,0:T(8,128)(2,1)S(1)} %get-tuple-element.68.refs_13_.act_two, f32[128,512]{1,0:T(8,128)S(1)} %get-tuple-element.53.w_three, bf16[384,256]{1,0:T(8,128)(2,1)S(1)} %get-tuple-element.47.refs_5_.first), custom_call_target="tpu_custom_call" | custom-call | flops 2000000000 | bytes 5439488 | tf_op jit(solution)/shard_map/pallas_call | solution.py:410
  26.7 0.8 %collective-permute-done.4 = f32[200,128]{1,0:T(8,128)S(1)} collective-permute-done((f32[200,128]{1,0:T(8,128)S(1)}, f32[200,128]{1,0:T(8,128)S(1)}, u32[]{:S(2)}, u32[]{:S(2)}) %collective-permute-start.4) | collective-permute-done | bytes 102432 | tf_op jit(solution)/shard_map/ppermute | solution.py:423
  27.5 1.6 %collective-permute-start.5 = (f32[200,128]{1,0:T(8,128)S(1)}, f32[200,128]{1,0:T(8,128)S(1)}, u32[]{:S(2)}, u32[]{:S(2)}) collective-permute-start(f32[200,128]{1,0:T(8,128)S(1)} %slice_add_fusion.1), channel_id=1, source_target_pairs={{0,4},{4,0},{8,12},{12,8},{16,20},{20,16},{24,28},{28,24},{1,5},{5... | collective-permute-start | bytes 307208 | tf_op jit(solution)/shard_map/ppermute | solution.py:423
  29.1 2.7 %collective-permute-start.9 = (f32[192,128]{1,0:T(8,128)S(1)}, f32[192,128]{1,0:T(8,128)S(1)}, u32[]{:S(2)}, u32[]{:S(2)}) collective-permute-start(f32[192,128]{1,0:T(8,128)S(1)} %slice_add_fusion), channel_id=1, source_target_pairs={{0,16},{4,20},{8,24},{12,28},{16,0},{20,4},{24,8},{28,12},{1,17},{... | collective-permute-start | bytes 294920 | tf_op jit(solution)/shard_map/ppermute | solution.py:423
  31.8 1.8 %shard_map.213 = bf16[128,512]{1,0:T(8,128)(2,1)} custom-call(f32[512,128]{1,0:T(8,128)S(1)} %get-tuple-element.64.refs_0_, f32[512,128]{1,0:T(8,128)S(1)} %get-tuple-element.65.refs_1_, f32[512,128]{1,0:T(8,128)S(1)} %get-tuple-element.66.refs_2_, bf16[256,256]{1,0:T(8,128)(2,1)S(1)} %get-tuple-element.48.refs_6_.refs_3_, ...), custom_call_target="tpu_custom_call" | custom-call | flops 1000000000 | bytes 9441280 | tf_op jit(solution)/shard_map/pallas_call | solution.py:410
  34.2 1.6 %collective-permute-done.9 = f32[192,128]{1,0:T(8,128)S(1)} collective-permute-done((f32[192,128]{1,0:T(8,128)S(1)}, f32[192,128]{1,0:T(8,128)S(1)}, u32[]{:S(2)}, u32[]{:S(2)}) %collective-permute-start.9) | collective-permute-done | bytes 98336 | tf_op jit(solution)/shard_map/ppermute | solution.py:423
  35.8 1.6 %collective-permute-start.10 = (f32[192,128]{1,0:T(8,128)S(1)}, f32[192,128]{1,0:T(8,128)S(1)}, u32[]{:S(2)}, u32[]{:S(2)}) collective-permute-start(f32[192,128]{1,0:T(8,128)S(1)} %add.33), channel_id=1, source_target_pairs={{0,2},{1,3},{2,0},{3,1},{4,6},{5,7},{6,4},{7,5},{8,10},{9,11},{10,... | collective-permute-start | bytes 294920 | tf_op jit(solution)/shard_map/ppermute | solution.py:423
  37.3 1.0 %collective-permute-done.7 = f32[200,128]{1,0:T(8,128)S(1)} collective-permute-done((f32[200,128]{1,0:T(8,128)S(1)}, f32[200,128]{1,0:T(8,128)S(1)}, u32[]{:S(2)}, u32[]{:S(2)}) %collective-permute-start.7) | collective-permute-done | bytes 102432 | tf_op jit(solution)/shard_map/ppermute | solution.py:423
  38.4 1.5 %collective-permute-start.8 = (f32[200,128]{1,0:T(8,128)S(1)}, f32[200,128]{1,0:T(8,128)S(1)}, u32[]{:S(2)}, u32[]{:S(2)}) collective-permute-start(f32[200,128]{1,0:T(8,128)S(1)} %add.31), channel_id=1, source_target_pairs={{0,16},{4,20},{8,24},{12,28},{16,0},{20,4},{24,8},{28,12},{1,17},{... | collective-permute-start | bytes 307208 | tf_op jit(solution)/shard_map/ppermute | solution.py:423
  40.5 0.8 %collective-permute-start.11 = (f32[192,128]{1,0:T(8,128)S(1)}, f32[192,128]{1,0:T(8,128)S(1)}, u32[]{:S(2)}, u32[]{:S(2)}) collective-permute-start(f32[192,128]{1,0:T(8,128)S(1)} %add.34), channel_id=1, source_target_pairs={{0,4},{4,0},{8,12},{12,8},{16,20},{20,16},{24,28},{28,24},{1,5},{5... | collective-permute-start | bytes 294920 | tf_op jit(solution)/shard_map/ppermute | solution.py:423
  41.3 3.9 %collective-permute-done.11 = f32[192,128]{1,0:T(8,128)S(1)} collective-permute-done((f32[192,128]{1,0:T(8,128)S(1)}, f32[192,128]{1,0:T(8,128)S(1)}, u32[]{:S(2)}, u32[]{:S(2)}) %collective-permute-start.11) | collective-permute-done | bytes 98336 | tf_op jit(solution)/shard_map/ppermute | solution.py:423
  45.3 1.4 %collective-permute-done.12.other = f32[392,128]{1,0:T(8,128)S(1)} collective-permute-done((f32[392,128]{1,0:T(8,128)S(1)}, f32[392,128]{1,0:T(8,128)S(1)}, u32[]{:S(2)}, u32[]{:S(2)}) %collective-permute-start.12) | collective-permute-done | bytes 200736 | tf_op jit(solution)/shard_map/ppermute | solution.py:423
  46.7 0.8 %shard_map.214 = (f32[128,128]{1,0:T(8,128)}, f32[1,128]{1,0:T(1,128)}, f32[128,128]{1,0:T(8,128)}, f32[1,128]{1,0:T(1,128)}, f32[128,512]{1,0:T(8,128)}) custom-call(f32[392,128]{1,0:T(8,128)S(1)} %pad_maximum_fusion.mine, f32[392,128]{1,0:T(8,128)S(1)} %collective-permute-done.12.other), custom_call_target="tpu_custom_call" | custom-call | bytes 795648 | tf_op jit(solution)/shard_map/pallas_call | solution.py:410
  (24 shorter events, 1.9 us)
Async XLA Ops:
  0.6 4.7 %collective-permute-start = (s32[1,128]{1,0:T(1,128)}, s32[1,128]{1,0:T(1,128)S(1)}, u32[]{:S(2)}, u32[]{:S(2)}) collective-permute-start(s32[1,128]{1,0:T(1,128)} %refs_12_.1), channel_id=1, source_target_pairs={{0,4},{4,0},{8,12},{12,8},{16,20},{20,16},{24,28},{28,24},{1,5},{5... | collective-permute-start | bytes 1544 | tf_op jit(solution)/shard_map/ppermute | solution.py:423
  5.4 3.6 %collective-permute-start.1 = (s32[2,128]{1,0:T(2,128)S(1)}, s32[2,128]{1,0:T(2,128)S(1)}, u32[]{:S(2)}, u32[]{:S(2)}) collective-permute-start(s32[2,128]{1,0:T(2,128)S(1)} %pad_add_fusion.2), channel_id=1, source_target_pairs={{0,8},{4,12},{8,0},{12,4},{16,24},{20,28},{24,16},{28,20},{1,9},{5... | collective-permute-start | bytes 3080 | tf_op jit(solution)/shard_map/ppermute | solution.py:423
  9.0 4.6 %collective-permute-start.2 = (s32[4,128]{1,0:T(4,128)S(1)}, s32[4,128]{1,0:T(4,128)S(1)}, u32[]{:S(2)}, u32[]{:S(2)}) collective-permute-start(s32[4,128]{1,0:T(4,128)S(1)} %pad_add_fusion.1), channel_id=1, source_target_pairs={{0,16},{4,20},{8,24},{12,28},{16,0},{20,4},{24,8},{28,12},{1,17},{... | collective-permute-start | bytes 6152 | tf_op jit(solution)/shard_map/ppermute | solution.py:423
  19.3 1.5 %collective-permute-start.3 = (f32[392,128]{1,0:T(8,128)S(1)}, f32[392,128]{1,0:T(8,128)S(1)}, u32[]{:S(2)}, u32[]{:S(2)}) collective-permute-start(f32[392,128]{1,0:T(8,128)S(1)} %get-tuple-element.63), channel_id=1, source_target_pairs={{0,1},{1,0},{2,3},{3,2},{4,5},{5,4},{6,7},{7,6},{8,9},{9,8},{10,11... | collective-permute-start | bytes 602120 | tf_op jit(solution)/shard_map/ppermute | solution.py:423
  20.9 8.2 %collective-permute-start.6 = (f32[192,128]{1,0:T(8,128)S(1)}, f32[192,128]{1,0:T(8,128)S(1)}, u32[]{:S(2)}, u32[]{:S(2)}) collective-permute-start(f32[192,128]{1,0:T(8,128)S(1)} %slice.9), channel_id=1, source_target_pairs={{0,8},{4,12},{8,0},{12,4},{16,24},{20,28},{24,16},{28,20},{1,9},{5... | collective-permute-start | bytes 294920 | tf_op jit(solution)/shard_map/ppermute | solution.py:423
  22.8 4.7 %collective-permute-start.4 = (f32[200,128]{1,0:T(8,128)S(1)}, f32[200,128]{1,0:T(8,128)S(1)}, u32[]{:S(2)}, u32[]{:S(2)}) collective-permute-start(f32[200,128]{1,0:T(8,128)S(1)} %slice.8), channel_id=1, source_target_pairs={{0,2},{1,3},{2,0},{3,1},{4,6},{5,7},{6,4},{7,5},{8,10},{9,11},{10,... | collective-permute-start | bytes 307208 | tf_op jit(solution)/shard_map/ppermute | solution.py:423
  27.5 6.1 %collective-permute-start.5 = (f32[200,128]{1,0:T(8,128)S(1)}, f32[200,128]{1,0:T(8,128)S(1)}, u32[]{:S(2)}, u32[]{:S(2)}) collective-permute-start(f32[200,128]{1,0:T(8,128)S(1)} %slice_add_fusion.1), channel_id=1, source_target_pairs={{0,4},{4,0},{8,12},{12,8},{16,20},{20,16},{24,28},{28,24},{1,5},{5... | collective-permute-start | bytes 307208 | tf_op jit(solution)/shard_map/ppermute | solution.py:423
  29.1 6.6 %collective-permute-start.9 = (f32[192,128]{1,0:T(8,128)S(1)}, f32[192,128]{1,0:T(8,128)S(1)}, u32[]{:S(2)}, u32[]{:S(2)}) collective-permute-start(f32[192,128]{1,0:T(8,128)S(1)} %slice_add_fusion), channel_id=1, source_target_pairs={{0,16},{4,20},{8,24},{12,28},{16,0},{20,4},{24,8},{28,12},{1,17},{... | collective-permute-start | bytes 294920 | tf_op jit(solution)/shard_map/ppermute | solution.py:423
  33.6 4.7 %collective-permute-start.7 = (f32[200,128]{1,0:T(8,128)S(1)}, f32[200,128]{1,0:T(8,128)S(1)}, u32[]{:S(2)}, u32[]{:S(2)}) collective-permute-start(f32[200,128]{1,0:T(8,128)S(1)} %add.29), channel_id=1, source_target_pairs={{0,8},{4,12},{8,0},{12,4},{16,24},{20,28},{24,16},{28,20},{1,9},{5... | collective-permute-start | bytes 307208 | tf_op jit(solution)/shard_map/ppermute | solution.py:423
  35.8 4.7 %collective-permute-start.10 = (f32[192,128]{1,0:T(8,128)S(1)}, f32[192,128]{1,0:T(8,128)S(1)}, u32[]{:S(2)}, u32[]{:S(2)}) collective-permute-start(f32[192,128]{1,0:T(8,128)S(1)} %add.33), channel_id=1, source_target_pairs={{0,2},{1,3},{2,0},{3,1},{4,6},{5,7},{6,4},{7,5},{8,10},{9,11},{10,... | collective-permute-start | bytes 294920 | tf_op jit(solution)/shard_map/ppermute | solution.py:423
  38.4 6.8 %collective-permute-start.8 = (f32[200,128]{1,0:T(8,128)S(1)}, f32[200,128]{1,0:T(8,128)S(1)}, u32[]{:S(2)}, u32[]{:S(2)}) collective-permute-start(f32[200,128]{1,0:T(8,128)S(1)} %add.31), channel_id=1, source_target_pairs={{0,16},{4,20},{8,24},{12,28},{16,0},{20,4},{24,8},{28,12},{1,17},{... | collective-permute-start | bytes 307208 | tf_op jit(solution)/shard_map/ppermute | solution.py:423
  40.5 4.7 %collective-permute-start.11 = (f32[192,128]{1,0:T(8,128)S(1)}, f32[192,128]{1,0:T(8,128)S(1)}, u32[]{:S(2)}, u32[]{:S(2)}) collective-permute-start(f32[192,128]{1,0:T(8,128)S(1)} %add.34), channel_id=1, source_target_pairs={{0,4},{4,0},{8,12},{12,8},{16,20},{20,16},{24,28},{28,24},{1,5},{5... | collective-permute-start | bytes 294920 | tf_op jit(solution)/shard_map/ppermute | solution.py:423
  45.2 1.5 %collective-permute-start.12 = (f32[392,128]{1,0:T(8,128)S(1)}, f32[392,128]{1,0:T(8,128)S(1)}, u32[]{:S(2)}, u32[]{:S(2)}) collective-permute-start(f32[392,128]{1,0:T(8,128)S(1)} %pad_maximum_fusion.mine), channel_id=1, source_target_pairs={{0,1},{1,0},{2,3},{3,2},{4,5},{5,4},{6,7},{7,6},{8,9},{9,8},{10,11... | collective-permute-start | bytes 602120 | tf_op jit(solution)/shard_map/ppermute | solution.py:423
